TPU v7x, 1024 devices: a whole 4x4x32 slice. The times are simulated.
1024 devices in a mesh: dp: 4 (over x), half: 4 (over y), own: 64 (over z, core).
Axes of the slice: x: 4, y: 4, z: 32, core: 2. Of those that a mesh axis runs over, the one named last changes fastest.
Arguments:
- grad_parts: bfloat16 [4, 132, 1024, 1024], P('dp', None, ('half', 'own')), may hold values from -6 to 6
- owner_table: int32 [132, 1], replicated, may hold values from 0 to 63; in each aligned block of 132 rows (0 to 131, 132 to 263, ...) at most 4 rows name the same one
- left_basis: bfloat16 [256, 1024, 1024], P(('half', 'own')), may hold values from -0.1875 to 0.1875
- right_basis: bfloat16 [256, 1024, 1024], P(('half', 'own')), may hold values from -0.1875 to 0.1875
- first_moment: bfloat16 [256, 1024, 1024], P(('half', 'own'), 'dp'), may hold values from -6 to 6
- second_moment: bfloat16 [256, 1024, 1024], P(('half', 'own'), 'dp'), may hold values from 0.5 to 8
Outputs:
- update: bfloat16 [132, 1024, 1024], P(None, ('half', 'own'), 'dp')
Inputs may be any that keep to these rules, and one draw needn't show every extreme that they name: `owner_table`: every owner index is named by at least one block and by at most 4 blocks; some owner is named by exactly 4 blocks.
All inputs are finite; a program needn't handle non-finite values.
Results may differ from a plain program's by a relative error of at most 0.013.
Values may be sent and summed in bfloat16 or wider, within the bound.
No kernel may reach another device: no remote copies, remote signals or barrier semaphores. Data moves between devices by JAX's collectives and lax.ppermute only.
A program may use at most 128 MiB of HBM per device.

v0:
```python
import jax
import jax.numpy as jnp
from jax import lax
from jax.sharding import PartitionSpec as P

beta_first = 0.9
beta_second = 0.95
bias_first = 1.0 - 0.9**10
bias_second = 1.0 - 0.95**10
epsilon = 1e-08


def split_up(array, dim, length):
    before, after = (array.shape[:dim], array.shape[dim + 1 :])
    return jnp.moveaxis(array.reshape(*before, length, -1, *after), dim, 0)


def sum_at_owner(array, axis, dim):
    blocks = split_up(array, dim, lax.axis_size(axis))
    arrived = lax.all_to_all(blocks, axis, split_axis=0, concat_axis=0, tiled=True)
    return arrived.astype(jnp.float32).sum(axis=0)


def laid_out(blocks, dim):
    blocks = jnp.moveaxis(blocks, 0, dim)
    lengths = blocks.shape
    return blocks.reshape(*lengths[:dim], lengths[dim] * lengths[dim + 1], *lengths[dim + 2 :])


def joined_exchange(array, axis, axes, splits, concats):
    sizes = [lax.axis_size(a) for a in axes]
    blocks = split_up(array, splits[0], sizes[0])
    blocks = jnp.moveaxis(split_up(blocks, splits[1] + 1, sizes[1]), 0, 1)
    inside = blocks.shape[2:]
    blocks = blocks.reshape(-1, *inside)
    blocks = lax.all_to_all(blocks, axis, split_axis=0, concat_axis=0, tiled=True)
    blocks = laid_out(blocks.reshape(*sizes, *inside), concats[0] + 1)
    return laid_out(blocks, concats[1])


def from_everyone(array, axis):
    length = lax.axis_size(axis)
    return lax.all_to_all(
        jnp.broadcast_to(array[None], (length, *array.shape)), axis, 0, 0, tiled=True
    )


def gather_directly(array, axis, dim):
    blocks = from_everyone(array, axis)
    return laid_out(blocks, dim)


def slot_select(owner_table, owner_count, slot_count):
    owner_ids = owner_table[:, 0]
    positions = jnp.arange(owner_ids.shape[0], dtype=jnp.int32)
    shared = (owner_ids[:, None] == owner_ids[None, :]) & (positions[None, :] < positions[:, None])
    ranking = jnp.sum(shared.astype(jnp.int32), axis=1)
    slot_ids = ranking * owner_count + owner_ids
    slot_range = jnp.arange(slot_count, dtype=jnp.int32)
    return (slot_range[:, None] == slot_ids[None, :]).astype(jnp.bfloat16)


def local(grad_parts, owner_table, left_basis, right_basis, first_moment, second_moment):
    halves = lax.axis_size("half")
    owners = lax.axis_size("own")
    replicas = lax.axis_size("dp")
    block_count = grad_parts.shape[1]
    piece_rows = grad_parts.shape[2]
    block_width = grad_parts.shape[3]
    quarter = block_width // replicas
    offset = lax.axis_index("dp") * quarter
    summed = sum_at_owner(grad_parts[0].astype(jnp.float32).astype(jnp.bfloat16), "dp", 2)
    selector = slot_select(owner_table, owners, halves * owners)
    flat_grad = summed.astype(jnp.bfloat16).reshape(block_count, piece_rows * quarter)
    packed = jnp.dot(selector, flat_grad, preferred_element_type=jnp.float32).astype(jnp.bfloat16)
    packed = packed.reshape(halves, owners, piece_rows, quarter)
    arrived = joined_exchange(packed, ("half", "own"), ("half", "own"), (0, 1), (0, 1))
    grad_block = arrived.reshape(block_width, quarter)
    left_matrix = left_basis[0]
    right_matrix = right_basis[0]
    right_rows = lax.dynamic_slice_in_dim(right_matrix, offset, quarter, 0)
    left_cols = left_matrix
    product = lax.dot_general(
        left_cols, grad_block, (((0,), (0,)), ((), ())), preferred_element_type=jnp.float32
    )
    rotated = sum_at_owner(
        jnp.dot(
            product.astype(jnp.bfloat16), right_rows, preferred_element_type=jnp.float32
        ).astype(jnp.bfloat16),
        "dp",
        0,
    )
    first_new = beta_first * first_moment[0].astype(jnp.float32) + (1.0 - beta_first) * rotated
    second_new = (
        beta_second * second_moment[0].astype(jnp.float32) + (1.0 - beta_second) * rotated * rotated
    )
    direction = (first_new / bias_first / (jnp.sqrt(second_new / bias_second) + epsilon)).astype(
        jnp.bfloat16
    )
    partial_cols = lax.dot_general(
        gather_directly(direction, "dp", 0),
        right_rows,
        (((1,), (1,)), ((), ())),
        preferred_element_type=jnp.float32,
    )
    left_cols = left_matrix
    update_block = jnp.dot(
        left_cols, partial_cols.astype(jnp.bfloat16), preferred_element_type=jnp.float32
    )
    outgoing = update_block.astype(jnp.bfloat16).reshape(halves, owners, piece_rows, quarter)
    returned = joined_exchange(outgoing, ("half", "own"), ("half", "own"), (0, 1), (0, 1))
    flat_back = returned.reshape(halves * owners, piece_rows * quarter)
    placed = lax.dot_general(
        selector, flat_back, (((0,), (0,)), ((), ())), preferred_element_type=jnp.float32
    )
    return placed.astype(jnp.bfloat16).reshape(block_count, piece_rows, quarter)


def solution(mesh):
    return jax.shard_map(
        local,
        mesh=mesh,
        in_specs=(
            P("dp", None, ("half", "own"), None),
            P(),
            P(("half", "own"), None, None),
            P(("half", "own"), None, None),
            P(("half", "own"), "dp", None),
            P(("half", "own"), "dp", None),
        ),
        out_specs=P(None, ("half", "own"), "dp"),
        check_vma=False,
    )
```

profile of v0, /device:TPU:1, one launch (start us, length us, event | category | flops | bytes accessed | tf_op | source)
XLA Modules:
  0.0 272.1 jit_solution(5517520422453882100)
XLA Ops:
  0.0 2.6 reshape.63
  2.7 1.4 copy.17
  4.1 4.8 %all-to-all-start = ((bf16[4,132,4,256]{3,2,1,0:T(4,128)(2,1)}), bf16[4,132,4,256]{3,2,1,0:T(4,128)(2,1)S(1)}, u32[]{:S(2)}, u32[]{:S(2)}) async-start(bf16[4,132,4,256]{3,2,1,0:T(4,128)(2,1)} %copy.17), calls=%async_computation | async-start | bytes 2162688 | tf_op jit(solution)/shard_map/all_to_all | solution.py:20
  8.9 0.2 convert_reduce_fusion.1
  9.1 9.7 %all-to-all-done = bf16[4,132,4,256]{3,2,1,0:T(4,128)(2,1)S(1)} async-done(((bf16[4,132,4,256]{3,2,1,0:T(4,128)(2,1)}), bf16[4,132,4,256]{3,2,1,0:T(4,128)(2,1)S(1)}, u32[]{:S(2)}, u32[]{:S(2)}) %all-to-all-start) | async-done | bytes 1081376 | tf_op jit(solution)/shard_map/all_to_all | solution.py:20
  18.8 0.7 reduce_sum.33
  19.7 0.3 convolution_convert_fusion.2
  20.0 1.2 reshape_transpose_transpose_reshape_reshape_reshape.6
  21.2 40.3 %all-to-all-start.1 = ((bf16[256,1,1,4,256]{4,3,2,1,0:T(4,128)(2,1)}), bf16[256,1,1,4,256]{4,3,2,1,0:T(4,128)(2,1)S(1)}, u32[]{:S(2)}, u32[]{:S(2)}) async-start(bf16[256,1,1,4,256]{4,3,2,1,0:T(4,128)(2,1)} %bitcast.3), calls=%async_computation.1 | async-start | bytes 1048576 | tf_op jit(solution)/shard_map/all_to_all | solution.py:36
  61.5 66.1 %all-to-all-done.1 = bf16[256,1,1,4,256]{4,3,2,1,0:T(4,128)(2,1)S(1)} async-done(((bf16[256,1,1,4,256]{4,3,2,1,0:T(4,128)(2,1)}), bf16[256,1,1,4,256]{4,3,2,1,0:T(4,128)(2,1)S(1)}, u32[]{:S(2)}, u32[]{:S(2)}) %all-to-all-start.1) | async-done | bytes 524320 | tf_op jit(solution)/shard_map/all_to_all | solution.py:36
  127.7 3.8 %convolution_convert_fusion = bf16[1024,1024]{1,0:T(8,128)(2,1)} fusion(bf16[1024,256]{1,0:T(8,128)(2,1)S(1)} %reshape_reshape.6, bf16[1,1024,1024]{2,1,0:T(8,128)(2,1)S(1)} %copy-done, bf16[1,1024,1024]{2,1,0:T(8,128)(2,1)} %param.9, s32[]{:T(128)S(6)} %select_n.3), kind=kOutput, calls=%fused_computation.5 | convolution fusion | flops 1075052544 | bytes 5242884 | tf_op jit(solution)/shard_map/dot_general | solution.py:87
  131.5 28.6 %all_to_all.25 = bf16[4,256,1024]{2,1,0:T(8,128)(2,1)S(1)} all-to-all(bf16[4,256,1024]{2,1,0:T(8,128)(2,1)} %bitcast.73), channel_id=1, replica_groups=mesh['dp'=4,'half'=4,'own'=64] {'dp'}, dimensions={0} | all-to-all | bytes 4194304 | tf_op jit(solution)/shard_map/all_to_all | solution.py:20
  160.1 0.4 convert_reduce_fusion
  160.5 0.6 copy-done.1
  161.1 0.2 copy-done.2
  161.3 0.8 fusion.26
  162.0 0.3 broadcast_in_dim.5
  162.3 29.3 %all_to_all.26 = bf16[4,256,1024]{2,1,0:T(8,128)(2,1)} all-to-all(bf16[4,256,1024]{2,1,0:T(8,128)(2,1)S(1)} %broadcast_in_dim.5), channel_id=1, replica_groups=mesh['dp'=4,'half'=4,'own'=64] {'dp'}, dimensions={0} | all-to-all | bytes 4194304 | tf_op jit(solution)/shard_map/all_to_all | solution.py:43
  191.6 4.0 %fusion.10 = bf16[1024,256]{0,1:T(8,128)(2,1)S(1)} fusion(bf16[1,1024,1024]{2,1,0:T(8,128)(2,1)S(1)} %copy-done, bf16[1024,1024]{1,0:T(8,128)(2,1)} %bitcast.72, bf16[1,1024,1024]{2,1,0:T(8,128)(2,1)} %param.9, s32[]{:T(128)S(6)} %select_n.3), kind=kOutput, calls=%fused_computation.11 | convolution fusion | flops 1074266112 | bytes 5242884 | tf_op jit(solution)/shard_map/dot_general | solution.py:107
  195.6 0.2 copy.19
  195.8 0.1 reshape_transpose_transpose_reshape_reshape_reshape.7
  195.9 74.9 %all_to_all.27 = bf16[256,1,1,4,256]{4,3,2,1,0:T(4,128)(2,1)S(1)} all-to-all(bf16[256,1,1,4,256]{4,3,2,1,0:T(4,128)(2,1)S(1)} %bitcast.75), channel_id=1, replica_groups=mesh['dp'=4,'half'=4,'own'=64] {'half','own'}, dimensions={0} | all-to-all | bytes 1048576 | tf_op jit(solution)/shard_map/all_to_all | solution.py:36
  270.9 0.3 convolution_convert_fusion.3
  271.2 0.8 reshape.62
  (11 shorter events, 0.4 us)
Async XLA Ops:
  0.0 127.7 %copy-start = (bf16[1,1024,1024]{2,1,0:T(8,128)(2,1)S(1)}, bf16[1,1024,1024]{2,1,0:T(8,128)(2,1)}, u32[]{:S(2)}) copy-start(bf16[1,1024,1024]{2,1,0:T(8,128)(2,1)} %param.8) | copy-start | bytes 6291460
  2.7 6.3 %copy-start.3 = (s32[132,1]{0,1:T(1,128)S(1)}, s32[132,1]{0,1:T(1,128)}, u32[]{:S(2)}) copy-start(s32[132,1]{0,1:T(1,128)} %param.7) | copy-start | bytes 1588
  4.1 14.8 %all-to-all-start = ((bf16[4,132,4,256]{3,2,1,0:T(4,128)(2,1)}), bf16[4,132,4,256]{3,2,1,0:T(4,128)(2,1)S(1)}, u32[]{:S(2)}, u32[]{:S(2)}) async-start(bf16[4,132,4,256]{3,2,1,0:T(4,128)(2,1)} %copy.17), calls=%async_computation | async-start | bytes 2162688 | tf_op jit(solution)/shard_map/all_to_all | solution.py:20
  21.2 106.4 %all-to-all-start.1 = ((bf16[256,1,1,4,256]{4,3,2,1,0:T(4,128)(2,1)}), bf16[256,1,1,4,256]{4,3,2,1,0:T(4,128)(2,1)S(1)}, u32[]{:S(2)}, u32[]{:S(2)}) async-start(bf16[256,1,1,4,256]{4,3,2,1,0:T(4,128)(2,1)} %bitcast.3), calls=%async_computation.1 | async-start | bytes 1048576 | tf_op jit(solution)/shard_map/all_to_all | solution.py:36
  160.1 1.0 copy-start.1
  160.1 1.2 copy-start.2
where the time goes:
time: 273 us; the launch traced here: 272 us
  blocking collectives  133 us (49%)
  waiting for transfers between devices  75.8 us (28%)
  starting transfers between devices  45.1 us (17%)
  matrix products  8.32 us (3%)
  local copies, waits for them, and re-layouts  7.81 us (3%)
    all_to_all x1, blocking collectives, joined_exchange(): lax.all_to_all(blocks, axis, split_axis=0, concat_axis=0, tiled=True)  74.9 us
    all_to_all x1, waiting for transfers between devices, joined_exchange(): lax.all_to_all(blocks, axis, split_axis=0, concat_axis=0, tiled=True)  66.1 us
    all_to_all x1, starting transfers between devices, joined_exchange(): lax.all_to_all(blocks, axis, split_axis=0, concat_axis=0, tiled=True)  40.3 us
    all_to_all x1, blocking collectives, from_everyone(): lax.all_to_all(jnp.broadcast_to(array[None], (length, *array.shape)), axi...  29.3 us
    all_to_all x1, blocking collectives, sum_at_owner(): lax.all_to_all(blocks, axis, split_axis=0, concat_axis=0, tiled=True)  28.6 us
    all_to_all x1, waiting for transfers between devices, sum_at_owner(): lax.all_to_all(blocks, axis, split_axis=0, concat_axis=0, tiled=True)  9.71 us
  transfers between devices with their start and end apart: 2, of which 2 were waited for; matrix products, arithmetic and copies ran while one was open for 0% of the time, Pallas kernels for 0%

commit v1 on v0

v1 whole, which is shorter than its diff:
```python
import jax
import jax.numpy as jnp
from jax import lax
from jax.sharding import Mesh, PartitionSpec as P

beta_first = 0.9
beta_second = 0.95
bias_first = 1.0 - 0.9**10
bias_second = 1.0 - 0.95**10
epsilon = 1e-08
cores = 2


def exchange(array, axes):
    return lax.all_to_all(array, axes, split_axis=0, concat_axis=0, tiled=True)


def slot_select(owner_table, owner_count, ranks):
    owner_ids = owner_table[:, 0]
    positions = jnp.arange(owner_ids.shape[0], dtype=jnp.int32)
    shared = (owner_ids[:, None] == owner_ids[None, :]) & (positions[None, :] < positions[:, None])
    ranking = jnp.sum(shared.astype(jnp.int32), axis=1)
    places = (ranking * cores + owner_ids % cores) * (owner_count // cores) + owner_ids // cores
    slot_range = jnp.arange(owner_count * ranks, dtype=jnp.int32)
    return (slot_range[:, None] == places[None, :]).astype(jnp.bfloat16)


def local(grad_parts, owner_table, left_basis, right_basis, first_moment, second_moment):
    replicas = lax.axis_size("dp")
    halves = lax.axis_size("half")
    depth = lax.axis_size("z")
    owners = depth * cores
    _, block_count, piece_rows, width = grad_parts.shape
    quarter = width // replicas
    left = left_basis[0]
    right = right_basis[0]

    parts = jnp.moveaxis(grad_parts[0].reshape(block_count, piece_rows, replicas, quarter), 2, 0)
    summed = exchange(parts, "dp").astype(jnp.float32).sum(axis=0).astype(jnp.bfloat16)

    selector = slot_select(owner_table, owners, halves)
    packed = jnp.dot(
        selector,
        summed.reshape(block_count, piece_rows * quarter),
        preferred_element_type=jnp.float32,
    ).astype(jnp.bfloat16)
    packed = packed.reshape(halves * cores, depth, piece_rows, quarter)
    arrived = exchange(packed, ("half", "core"))
    arrived = exchange(jnp.moveaxis(arrived, 1, 0), "z")
    arrived = arrived.reshape(depth, halves, cores, piece_rows, quarter)
    block = jnp.moveaxis(arrived, 1, 0).reshape(width, quarter)

    projected = lax.dot_general(
        left, block, (((0,), (0,)), ((), ())), preferred_element_type=jnp.float32
    ).astype(jnp.bfloat16)
    projected = exchange(projected.reshape(replicas, quarter, quarter), "dp")
    rotated = lax.dot_general(
        jnp.moveaxis(projected, 0, 1).reshape(quarter, width),
        right,
        (((1,), (0,)), ((), ())),
        preferred_element_type=jnp.float32,
    )
    first_new = beta_first * first_moment[0].astype(jnp.float32) + (1.0 - beta_first) * rotated
    second_new = (
        beta_second * second_moment[0].astype(jnp.float32) + (1.0 - beta_second) * rotated * rotated
    )
    direction = (first_new / bias_first / (jnp.sqrt(second_new / bias_second) + epsilon)).astype(
        jnp.bfloat16
    )
    back = lax.dot_general(
        direction, right, (((1,), (1,)), ((), ())), preferred_element_type=jnp.float32
    ).astype(jnp.bfloat16)
    back = exchange(jnp.moveaxis(back.reshape(quarter, replicas, quarter), 1, 0), "dp")
    update = jnp.dot(left, back.reshape(width, quarter), preferred_element_type=jnp.float32)

    outgoing = update.astype(jnp.bfloat16).reshape(halves, depth, cores, piece_rows, quarter)
    outgoing = jnp.moveaxis(outgoing, 1, 0).reshape(depth, halves * cores, piece_rows, quarter)
    returned = exchange(outgoing, "z")
    returned = exchange(jnp.moveaxis(returned, 1, 0), ("half", "core"))
    placed = lax.dot_general(
        selector,
        returned.reshape(halves * owners, piece_rows * quarter),
        (((0,), (0,)), ((), ())),
        preferred_element_type=jnp.float32,
    )
    return placed.astype(jnp.bfloat16).reshape(block_count, piece_rows, quarter)


def solution(mesh):
    replicas, halves, owners = (mesh.shape[axis] for axis in ("dp", "half", "own"))
    fine = Mesh(
        mesh.devices.reshape(replicas, halves, owners // cores, cores), ("dp", "half", "z", "core")
    )
    slots = ("half", "z", "core")
    return jax.shard_map(
        local,
        mesh=fine,
        in_specs=(
            P("dp", None, slots, None),
            P(),
            P(slots, None, None),
            P(slots, None, None),
            P(slots, "dp", None),
            P(slots, "dp", None),
        ),
        out_specs=P(None, slots, "dp"),
        check_vma=False,
    )
```

time: 273 us -> 246 us (0.901)
  blocking collectives: 133 us -> 215 us
  waiting for transfers between devices: 75.8 us -> 9.7 us
  starting transfers between devices: 45.1 us -> 4.84 us
    all_to_all x3 -> x6, blocking collectives: 133 us -> 215 us  [exchange(): return lax.all_to_all(array, axes, split_axis=0, concat_axis=0, tiled=True)]
    all_to_all x2 -> x1, waiting for transfers between devices: 75.8 us -> 9.7 us  [exchange(): return lax.all_to_all(array, axes, split_axis=0, concat_axis=0, tiled=True)]
    all_to_all x2 -> x1, starting transfers between devices: 45.1 us -> 4.84 us  [exchange(): return lax.all_to_all(array, axes, split_axis=0, concat_axis=0, tiled=True)]
    dot_general x4 -> x5, matrix products: 8.32 us -> 6.66 us  [the longest x1 4.59 us: local(): lax.dot_general(direction, right, (((1,), (1,)), ((), ())), preferred_ele...]
  transfers between devices with their start and end apart: 2 -> 1, of which waited for: 2 -> 1; matrix products, arithmetic and copies ran while one was open for 0% -> 0% of each run, Pallas kernels for 0% -> 0%
where the time goes in v1:
time: 246 us; the launch traced here: 245 us
  blocking collectives  215 us (87%)
  waiting for transfers between devices  9.7 us (4%)
  local copies, waits for them, and re-layouts  7.71 us (3%)
  matrix products  6.66 us (3%)
  starting transfers between devices  4.84 us (2%)
    all_to_all x6, blocking collectives, exchange(): return lax.all_to_all(array, axes, split_axis=0, concat_axis=0, tiled=True)  215 us
    all_to_all x1, waiting for transfers between devices, exchange(): return lax.all_to_all(array, axes, split_axis=0, concat_axis=0, tiled=True)  9.7 us
  transfers between devices with their start and end apart: 1, of which 1 were waited for; matrix products, arithmetic and copies ran while one was open for 0% of the time, Pallas kernels for 0%

profile of v1, /device:TPU:1, one launch (start us, length us, event | category | flops | bytes accessed | tf_op | source)
XLA Modules:
  0.0 245.1 jit_solution(18057124421631675467)
XLA Ops:
  0.0 2.6 %reshape.109 = bf16[132,4,4,256]{3,2,1,0:T(4,128)(2,1)S(1)} reshape(bf16[1,132,4,1024]{3,2,1,0:T(4,128)(2,1)} %param.6) | data formatting | bytes 2162688 | tf_op jit(solution)/shard_map/reshape;squeeze | solution.py:38
  2.7 1.4 copy.51
  4.1 4.8 %all-to-all-start = ((bf16[4,132,4,256]{3,2,1,0:T(4,128)(2,1)}), bf16[4,132,4,256]{3,2,1,0:T(4,128)(2,1)S(1)}, u32[]{:S(2)}, u32[]{:S(2)}) async-start(bf16[4,132,4,256]{3,2,1,0:T(4,128)(2,1)} %copy.51), calls=%async_computation | async-start | bytes 2162688 | tf_op jit(solution)/shard_map/all_to_all | solution.py:15
  8.9 0.2 convert_reduce_fusion
  9.1 9.7 %all-to-all-done = bf16[4,132,4,256]{3,2,1,0:T(4,128)(2,1)S(1)} async-done(((bf16[4,132,4,256]{3,2,1,0:T(4,128)(2,1)}), bf16[4,132,4,256]{3,2,1,0:T(4,128)(2,1)S(1)}, u32[]{:S(2)}, u32[]{:S(2)}) %all-to-all-start) | async-done | bytes 1081376 | tf_op jit(solution)/shard_map/all_to_all | solution.py:15
  18.8 0.7 reduce_sum.22
  19.7 0.3 convolution_convert_fusion
  20.0 0.4 reshape.98
  20.4 25.7 %all_to_all.35 = bf16[8,32,4,256]{3,2,1,0:T(4,128)(2,1)S(1)} all-to-all(bf16[8,32,4,256]{3,2,1,0:T(4,128)(2,1)S(1)} %reshape.98), channel_id=1, replica_groups=mesh['dp'=4,'half'=4,'z'=32,'core'=2] {'half','core'}, dimensions={0} | all-to-all | bytes 1048576 | tf_op jit(solution)/shard_map/all_to_all | solution.py:15
  46.1 0.3 copy.52
  46.4 86.9 %all_to_all.36 = bf16[32,8,4,256]{3,2,1,0:T(4,128)(2,1)S(1)} all-to-all(bf16[32,8,4,256]{3,2,1,0:T(4,128)(2,1)S(1)} %copy.52), channel_id=1, replica_groups=mesh['dp'=4,'half'=4,'z'=32,'core'=2] {'z'}, dimensions={0} | all-to-all | bytes 1048576 | tf_op jit(solution)/shard_map/all_to_all | solution.py:15
  133.3 0.3 copy.53
  133.6 0.4 copy.54
  134.1 0.7 fusion.8
  134.9 10.3 %all_to_all.37 = bf16[4,256,256]{1,2,0:T(8,128)(2,1)S(1)} all-to-all(bf16[4,256,256]{1,2,0:T(8,128)(2,1)S(1)} %bitcast.81), channel_id=1, replica_groups=mesh['dp'=4,'half'=4,'z'=32,'core'=2] {'dp'}, dimensions={0} | all-to-all | bytes 1048576 | tf_op jit(solution)/shard_map/all_to_all | solution.py:15
  145.2 4.6 %fusion.14 = bf16[256,1024]{1,0:T(8,128)(2,1)S(1)} fusion(bf16[1,1024,1024]{2,1,0:T(8,128)(2,1)} %param.9, bf16[1,256,1024]{2,1,0:T(8,128)(2,1)} %param.11, bf16[1,256,1024]{2,1,0:T(8,128)(2,1)} %param.10, bf16[256,1024]{0,1:T(8,128)(2,1)S(1)} %bitcast.90), kind=kOutput, calls=%fused_computation.11 | convolution fusion | flops 1077673984 | bytes 4194304 | tf_op jit(solution)/shard_map/dot_general | solution.py:70
  149.8 9.3 %all_to_all.38 = bf16[4,256,256]{2,1,0:T(8,128)(2,1)S(1)} all-to-all(bf16[4,256,256]{2,1,0:T(8,128)(2,1)S(1)} %bitcast.82), channel_id=1, replica_groups=mesh['dp'=4,'half'=4,'z'=32,'core'=2] {'dp'}, dimensions={0} | all-to-all | bytes 1048576 | tf_op jit(solution)/shard_map/all_to_all | solution.py:15
  159.2 0.8 fusion.17
  160.0 0.2 copy.57
  160.4 0.4 copy.59
  160.8 62.8 %all_to_all.39 = bf16[32,8,4,256]{3,2,1,0:T(4,128)(2,1)S(1)} all-to-all(bf16[32,8,4,256]{3,2,1,0:T(4,128)(2,1)S(1)} %copy.59), channel_id=1, replica_groups=mesh['dp'=4,'half'=4,'z'=32,'core'=2] {'z'}, dimensions={0} | all-to-all | bytes 1048576 | tf_op jit(solution)/shard_map/all_to_all | solution.py:15
  223.8 20.0 %all_to_all.40 = bf16[8,32,4,256]{3,2,1,0:T(4,128)(2,1)S(1)} all-to-all(bf16[8,32,4,256]{3,2,1,0:T(4,128)(2,1)S(1)} %copy.60), channel_id=1, replica_groups=mesh['dp'=4,'half'=4,'z'=32,'core'=2] {'half','core'}, dimensions={0} | all-to-all | bytes 1048576 | tf_op jit(solution)/shard_map/all_to_all | solution.py:15
  244.0 0.3 convolution_convert_fusion.1
  244.3 0.8 reshape.108
  (14 shorter events, 0.9 us)
Async XLA Ops:
  0.0 134.1 %copy-start = (bf16[1,1024,1024]{2,1,0:T(8,128)(2,1)S(1)}, bf16[1,1024,1024]{2,1,0:T(8,128)(2,1)}, u32[]{:S(2)}) copy-start(bf16[1,1024,1024]{2,1,0:T(8,128)(2,1)} %param.8) | copy-start | bytes 6291460
  2.7 6.3 %copy-start.1 = (s32[132,1]{0,1:T(1,128)S(1)}, s32[132,1]{0,1:T(1,128)}, u32[]{:S(2)}) copy-start(s32[132,1]{0,1:T(1,128)} %param.7) | copy-start | bytes 1588
  4.1 14.8 %all-to-all-start = ((bf16[4,132,4,256]{3,2,1,0:T(4,128)(2,1)}), bf16[4,132,4,256]{3,2,1,0:T(4,128)(2,1)S(1)}, u32[]{:S(2)}, u32[]{:S(2)}) async-start(bf16[4,132,4,256]{3,2,1,0:T(4,128)(2,1)} %copy.51), calls=%async_computation | async-start | bytes 2162688 | tf_op jit(solution)/shard_map/all_to_all | solution.py:15

commit v2 on v1

v2 whole, which is shorter than its diff:
```python
import jax
import jax.numpy as jnp
from jax import lax
from jax.experimental import pallas as pl
from jax.experimental.pallas import tpu as pltpu
from jax.sharding import PartitionSpec as P

beta_first = 0.9
beta_second = 0.95
bias_first = 1.0 - 0.9**10
bias_second = 1.0 - 0.95**10
epsilon = 1e-08
mib = 1 << 20


def exchange(array, axes):
    return lax.all_to_all(array, axes, split_axis=0, concat_axis=0, tiled=True)


def slot_select(owner_table, owner_count, slot_count):
    owner_ids = owner_table[:, 0]
    positions = jnp.arange(owner_ids.shape[0], dtype=jnp.int32)
    shared = (owner_ids[:, None] == owner_ids[None, :]) & (positions[None, :] < positions[:, None])
    ranking = jnp.sum(shared.astype(jnp.int32), axis=1)
    slot_ids = ranking * owner_count + owner_ids
    slot_range = jnp.arange(slot_count, dtype=jnp.int32)
    return (slot_range[:, None] == slot_ids[None, :]).astype(jnp.bfloat16)


def cut_columns(array, pieces):
    blocks, rows, width = array.shape
    part = width // pieces

    def kernel(source, target, done):
        copies = [
            pltpu.make_async_copy(
                source.at[:, :, pl.ds(p * part, part)], target.at[p], done.at[p]
            )
            for p in range(pieces)
        ]
        for copy in copies:
            copy.start()
        for copy in copies:
            copy.wait()

    return pl.pallas_call(
        kernel,
        out_shape=jax.ShapeDtypeStruct((pieces, blocks, rows, part), array.dtype),
        in_specs=[pl.BlockSpec(memory_space=pl.ANY)],
        out_specs=pl.BlockSpec(memory_space=pl.ANY),
        scratch_shapes=[pltpu.SemaphoreType.DMA((pieces,))],
        compiler_params=pltpu.CompilerParams(vmem_limit_bytes=mib),
        cost_estimate=pl.CostEstimate(
            flops=0, bytes_accessed=2 * array.size * array.dtype.itemsize, transcendentals=0
        ),
    )(array)


def turned_step(projected, right, first_moment, second_moment):
    pieces, rows, part = projected.shape
    width = pieces * part

    def kernel(projected, right, first_moment, second_moment, back, direction):
        left_rows = jnp.concatenate([projected[p] for p in range(pieces)], axis=1)
        for p in range(pieces):
            columns = pl.ds(p * part, part)
            rotated = jnp.dot(left_rows, right[:, columns], preferred_element_type=jnp.float32)
            first_new = (
                beta_first * first_moment[:, columns].astype(jnp.float32)
                + (1.0 - beta_first) * rotated
            )
            second_new = (
                beta_second * second_moment[:, columns].astype(jnp.float32)
                + (1.0 - beta_second) * rotated * rotated
            )
            direction[:, columns] = (
                first_new / bias_first / (jnp.sqrt(second_new / bias_second) + epsilon)
            ).astype(jnp.bfloat16)
        for p in range(pieces):
            back[p] = lax.dot_general(
                direction[...],
                right[pl.ds(p * part, part), :],
                (((1,), (1,)), ((), ())),
                preferred_element_type=jnp.float32,
            ).astype(jnp.bfloat16)

    return pl.pallas_call(
        kernel,
        out_shape=jax.ShapeDtypeStruct((pieces, rows, part), jnp.bfloat16),
        scratch_shapes=[pltpu.VMEM((rows, width), jnp.bfloat16)],
        compiler_params=pltpu.CompilerParams(vmem_limit_bytes=24 * mib),
        cost_estimate=pl.CostEstimate(
            flops=4 * rows * width * width,
            bytes_accessed=2 * (width * width + 4 * rows * width),
            transcendentals=2 * rows * width,
        ),
    )(projected, right, first_moment, second_moment)


def local(grad_parts, owner_table, left_basis, right_basis, first_moment, second_moment):
    replicas, halves, owners = (lax.axis_size(axis) for axis in ("dp", "half", "own"))
    _, block_count, piece_rows, width = grad_parts.shape
    quarter = width // replicas
    left = left_basis[0]

    parts = exchange(cut_columns(grad_parts[0], replicas), "dp")
    summed = parts.astype(jnp.float32).sum(axis=0).astype(jnp.bfloat16)

    selector = slot_select(owner_table, owners, halves * owners)
    packed = jnp.dot(
        selector,
        summed.reshape(block_count, piece_rows * quarter),
        preferred_element_type=jnp.float32,
    ).astype(jnp.bfloat16)
    block = exchange(packed.reshape(halves * owners, piece_rows, quarter), ("half", "own"))

    projected = lax.dot_general(
        left,
        block.reshape(width, quarter),
        (((0,), (0,)), ((), ())),
        preferred_element_type=jnp.float32,
    ).astype(jnp.bfloat16)
    projected = exchange(projected.reshape(replicas, quarter, quarter), "dp")
    back = turned_step(projected, right_basis[0], first_moment[0], second_moment[0])
    back = exchange(back, "dp")
    update = jnp.dot(left, back.reshape(width, quarter), preferred_element_type=jnp.float32)

    outgoing = update.astype(jnp.bfloat16).reshape(halves * owners, piece_rows, quarter)
    returned = exchange(outgoing, ("half", "own"))
    placed = lax.dot_general(
        selector,
        returned.reshape(halves * owners, piece_rows * quarter),
        (((0,), (0,)), ((), ())),
        preferred_element_type=jnp.float32,
    )
    return placed.astype(jnp.bfloat16).reshape(block_count, piece_rows, quarter)


def solution(mesh):
    slots = ("half", "own")
    return jax.shard_map(
        local,
        mesh=mesh,
        in_specs=(
            P("dp", None, slots, None),
            P(),
            P(slots, None, None),
            P(slots, None, None),
            P(slots, "dp", None),
            P(slots, "dp", None),
        ),
        out_specs=P(None, slots, "dp"),
        check_vma=False,
    )
```

time: 246 us -> 236 us (0.959)
  blocking collectives: 215 us -> 204 us
  Pallas kernels: 0 us -> 2.97 us
  matrix products: 6.66 us -> 4.03 us
    all_to_all x6 -> x4, blocking collectives: 215 us -> 204 us  [exchange(): return lax.all_to_all(array, axes, split_axis=0, concat_axis=0, tiled=True)]
    pallas_call x0 -> x2, Pallas kernels: none -> 2.97 us  [the longest x1 1.97 us: turned_step(): pl.pallas_call(kernel, out_shape=jax.ShapeDtypeStruct((pieces, rows, part...]
    unnamed x7 -> x14, local copies, waits for them, and re-layouts: 0.24 us -> 3.13 us
    dot_general x2 -> x1, matrix products: 5.33 us -> 2.65 us  [local(): lax.dot_general(left, block.reshape(width, quarter), (((0,), (0,)), ((),...]
    another operation x1 -> x0, local copies, waits for them, and re-layouts: 2.65 us -> none  [local(): grad_parts[0].reshape(block_count, piece_rows, replicas, quarter)]
where the time goes in v2:
time: 236 us
  blocking collectives  204 us (86%)
  waiting for transfers between devices  9.71 us (4%)
  local copies, waits for them, and re-layouts  8.95 us (4%)
  starting transfers between devices  4.85 us (2%)
  matrix products  4.03 us (2%)
  Pallas kernels  2.97 us (1%)
    all_to_all x4, blocking collectives, exchange(): return lax.all_to_all(array, axes, split_axis=0, concat_axis=0, tiled=True)  204 us
    all_to_all x1, waiting for transfers between devices, exchange(): return lax.all_to_all(array, axes, split_axis=0, concat_axis=0, tiled=True)  9.71 us
    all_to_all x1, starting transfers between devices, exchange(): return lax.all_to_all(array, axes, split_axis=0, concat_axis=0, tiled=True)  4.85 us
  transfers between devices with their start and end apart: 1, of which 1 were waited for; matrix products, arithmetic and copies ran while one was open for 0% of the time, Pallas kernels for 0%

profile of v2, /device:TPU:1, one launch (start us, length us, event | category | flops | bytes accessed | tf_op | source)
XLA Modules:
  0.0 235.8 jit_solution(15662509025106172134)
XLA Ops:
  0.0 1.4 copy-done.2
  1.4 1.0 shard_map.64
  2.4 4.9 %all-to-all-start = ((bf16[4,132,4,256]{3,2,1,0:T(4,128)(2,1)}), bf16[4,132,4,256]{3,2,1,0:T(4,128)(2,1)S(1)}, u32[]{:S(2)}, u32[]{:S(2)}) async-start(bf16[4,132,4,256]{3,2,1,0:T(4,128)(2,1)} %shard_map.64), calls=%async_computation | async-start | bytes 2162688 | tf_op jit(solution)/shard_map/all_to_all | solution.py:17
  7.3 0.2 convert_reduce_fusion
  7.5 9.7 %all-to-all-done = bf16[4,132,4,256]{3,2,1,0:T(4,128)(2,1)S(1)} async-done(((bf16[4,132,4,256]{3,2,1,0:T(4,128)(2,1)}), bf16[4,132,4,256]{3,2,1,0:T(4,128)(2,1)S(1)}, u32[]{:S(2)}, u32[]{:S(2)}) %all-to-all-start) | async-done | bytes 1081376 | tf_op jit(solution)/shard_map/all_to_all | solution.py:17
  17.2 0.7 reduce_sum.22
  17.9 0.1 pad
  18.0 0.3 convolution_convert_fusion
  18.3 0.4 reshape.34
  18.7 106.2 %all_to_all.25 = bf16[256,4,256]{2,1,0:T(4,128)(2,1)S(1)} all-to-all(bf16[256,4,256]{2,1,0:T(4,128)(2,1)S(1)} %reshape.34), channel_id=1, replica_groups=mesh['dp'=4,'half'=4,'own'=64] {'half','own'}, dimensions={0} | all-to-all | bytes 1048576 | tf_op jit(solution)/shard_map/all_to_all | solution.py:17
  124.9 0.9 reshape.35
  125.8 2.7 %fusion.13 = bf16[1024,256]{0,1:T(8,128)(2,1)} fusion(bf16[1024,256]{1,0:T(8,128)(2,1)} %reshape.35, bf16[1,1024,1024]{2,1,0:T(8,128)(2,1)S(1)} %copy-done), kind=kOutput, calls=%fused_computation.8 | convolution fusion | flops 537133056 | bytes 3145728 | tf_op jit(solution)/shard_map/dot_general | solution.py:117
  128.5 2.0 copy.11
  130.5 11.6 %all_to_all.26.projected = bf16[4,256,256]{2,1,0:T(8,128)(2,1)S(1)} all-to-all(bf16[4,256,256]{2,1,0:T(8,128)(2,1)} %bitcast.37), channel_id=1, replica_groups=mesh['dp'=4,'half'=4,'own'=64] {'dp'}, dimensions={0} | all-to-all | bytes 1048576 | tf_op jit(solution)/shard_map/all_to_all | solution.py:17
  142.1 1.6 copy-done.1
  143.7 2.0 shard_map.65
  145.7 11.6 %all_to_all.27 = bf16[4,256,256]{2,1,0:T(8,128)(2,1)S(1)} all-to-all(bf16[4,256,256]{2,1,0:T(8,128)(2,1)S(1)} %shard_map.65), channel_id=1, replica_groups=mesh['dp'=4,'half'=4,'own'=64] {'dp'}, dimensions={0} | all-to-all | bytes 1048576 | tf_op jit(solution)/shard_map/all_to_all | solution.py:17
  157.3 0.8 fusion.10
  158.1 0.2 copy.12
  158.3 0.1 reshape.38
  158.4 74.8 %all_to_all.28 = bf16[256,4,256]{2,1,0:T(4,128)(2,1)} all-to-all(bf16[256,4,256]{2,1,0:T(4,128)(2,1)S(1)} %reshape.38), channel_id=1, replica_groups=mesh['dp'=4,'half'=4,'own'=64] {'half','own'}, dimensions={0} | all-to-all | bytes 1048576 | tf_op jit(solution)/shard_map/all_to_all | solution.py:17
  233.3 1.3 copy.13
  234.6 0.3 convolution_convert_fusion.1
  234.9 0.8 reshape.40
  (12 shorter events, 0.1 us)
Async XLA Ops:
  0.0 125.8 %copy-start = (bf16[1,1024,1024]{2,1,0:T(8,128)(2,1)S(1)}, bf16[1,1024,1024]{2,1,0:T(8,128)(2,1)}, u32[]{:S(2)}) copy-start(bf16[1,1024,1024]{2,1,0:T(8,128)(2,1)} %param.8) | copy-start | bytes 6291460
  0.0 1.4 copy-start.2
  1.4 5.9 %copy-start.5 = (s32[132,1]{0,1:T(1,128)S(1)}, s32[132,1]{0,1:T(1,128)}, u32[]{:S(2)}) copy-start(s32[132,1]{0,1:T(1,128)} %param.7) | copy-start | bytes 1588
  2.4 14.8 %all-to-all-start = ((bf16[4,132,4,256]{3,2,1,0:T(4,128)(2,1)}), bf16[4,132,4,256]{3,2,1,0:T(4,128)(2,1)S(1)}, u32[]{:S(2)}, u32[]{:S(2)}) async-start(bf16[4,132,4,256]{3,2,1,0:T(4,128)(2,1)} %shard_map.64), calls=%async_computation | async-start | bytes 2162688 | tf_op jit(solution)/shard_map/all_to_all | solution.py:17
  125.8 16.3 %copy-start.3 = (bf16[1,256,1024]{2,1,0:T(8,128)(2,1)S(1)}, bf16[1,256,1024]{2,1,0:T(8,128)(2,1)}, u32[]{:S(2)}) copy-start(bf16[1,256,1024]{2,1,0:T(8,128)(2,1)} %param.10) | copy-start | bytes 1572868
  125.8 16.3 %copy-start.4 = (bf16[1,256,1024]{2,1,0:T(8,128)(2,1)S(1)}, bf16[1,256,1024]{2,1,0:T(8,128)(2,1)}, u32[]{:S(2)}) copy-start(bf16[1,256,1024]{2,1,0:T(8,128)(2,1)} %param.11) | copy-start | bytes 1572868
  142.1 1.6 copy-start.1

commit v3 on v2

v3 whole, which is shorter than its diff:
```python
import jax
import jax.numpy as jnp
from jax import lax
from jax.experimental import pallas as pl
from jax.experimental.pallas import tpu as pltpu
from jax.sharding import PartitionSpec as P

beta_first = 0.9
beta_second = 0.95
bias_first = 1.0 - 0.9**10
bias_second = 1.0 - 0.95**10
epsilon = 1e-08
mib = 1 << 20


def in_hbm(array):
    return pltpu.with_memory_space_constraint(array, pltpu.HBM)


def exchange(array, axes):
    return lax.all_to_all(array, axes, split_axis=0, concat_axis=0, tiled=True)


def slot_numbers(owner_table, owner_count):
    owner_ids = owner_table[:, 0]
    positions = jnp.arange(owner_ids.shape[0], dtype=jnp.int32)
    shared = (owner_ids[:, None] == owner_ids[None, :]) & (positions[None, :] < positions[:, None])
    ranking = jnp.sum(shared.astype(jnp.int32), axis=1)
    return ranking * owner_count + owner_ids


def cut_columns(array, pieces):
    blocks, rows, width = array.shape
    part = width // pieces

    def kernel(source, target, done):
        copies = [
            pltpu.make_async_copy(
                source.at[:, :, pl.ds(p * part, part)], target.at[p], done.at[p]
            )
            for p in range(pieces)
        ]
        for copy in copies:
            copy.start()
        for copy in copies:
            copy.wait()

    return pl.pallas_call(
        kernel,
        out_shape=jax.ShapeDtypeStruct((pieces, blocks, rows, part), array.dtype),
        in_specs=[pl.BlockSpec(memory_space=pltpu.HBM)],
        out_specs=pl.BlockSpec(memory_space=pltpu.HBM),
        scratch_shapes=[pltpu.SemaphoreType.DMA((pieces,))],
        compiler_params=pltpu.CompilerParams(vmem_limit_bytes=mib),
        cost_estimate=pl.CostEstimate(
            flops=0, bytes_accessed=2 * array.size * array.dtype.itemsize, transcendentals=0
        ),
    )(in_hbm(array))


def projected_columns(block, left, pieces):
    width, columns = block.shape
    part = width // pieces

    def kernel(block, left, out):
        for p in range(pieces):
            out[p] = lax.dot_general(
                block[...],
                left[:, pl.ds(p * part, part)],
                (((0,), (0,)), ((), ())),
                preferred_element_type=jnp.float32,
            ).astype(jnp.bfloat16)

    return pl.pallas_call(
        kernel,
        out_shape=jax.ShapeDtypeStruct((pieces, columns, part), jnp.bfloat16),
        compiler_params=pltpu.CompilerParams(vmem_limit_bytes=16 * mib),
        cost_estimate=pl.CostEstimate(
            flops=2 * width * width * columns,
            bytes_accessed=2 * (width * width + 2 * width * columns),
            transcendentals=0,
        ),
    )(block, left)


def turned_step(projected, right, first_moment, second_moment):
    pieces, part, rows = projected.shape
    width = pieces * part

    def kernel(projected, right, first, second, back, right_held, first_held, second_held, direction, done):
        cuts = [pl.ds(p * part, part) for p in range(pieces)]
        pairs = ((right, right_held), (first, first_held), (second, second_held))
        copies = [
            [
                pltpu.make_async_copy(source.at[:, cut], target.at[:, cut], done.at[n, p])
                for n, (source, target) in enumerate(pairs)
            ]
            for p, cut in enumerate(cuts)
        ]
        for group in copies:
            for copy in group:
                copy.start()
        turned = projected[...].reshape(width, rows)
        for cut, group in zip(cuts, copies):
            for copy in group:
                copy.wait()
            rotated = lax.dot_general(
                turned,
                right_held[:, cut],
                (((0,), (0,)), ((), ())),
                preferred_element_type=jnp.float32,
            )
            first_new = (
                beta_first * first_held[:, cut].astype(jnp.float32) + (1.0 - beta_first) * rotated
            )
            second_new = (
                beta_second * second_held[:, cut].astype(jnp.float32)
                + (1.0 - beta_second) * rotated * rotated
            )
            direction[:, cut] = (
                first_new / bias_first / (jnp.sqrt(second_new / bias_second) + epsilon)
            ).astype(jnp.bfloat16)
        for p, cut in enumerate(cuts):
            back[p] = lax.dot_general(
                direction[...],
                right_held[cut, :],
                (((1,), (1,)), ((), ())),
                preferred_element_type=jnp.float32,
            ).astype(jnp.bfloat16)

    here, far = pl.BlockSpec(memory_space=pltpu.VMEM), pl.BlockSpec(memory_space=pltpu.HBM)
    return pl.pallas_call(
        kernel,
        out_shape=jax.ShapeDtypeStruct((pieces, rows, part), jnp.bfloat16),
        in_specs=[here, far, far, far],
        out_specs=here,
        scratch_shapes=[
            pltpu.VMEM((width, width), jnp.bfloat16),
            pltpu.VMEM((rows, width), jnp.bfloat16),
            pltpu.VMEM((rows, width), jnp.bfloat16),
            pltpu.VMEM((rows, width), jnp.bfloat16),
            pltpu.SemaphoreType.DMA((3, pieces)),
        ],
        compiler_params=pltpu.CompilerParams(vmem_limit_bytes=16 * mib),
        cost_estimate=pl.CostEstimate(
            flops=4 * rows * width * width,
            bytes_accessed=2 * (width * width + 4 * rows * width),
            transcendentals=2 * rows * width,
        ),
    )(projected, *(in_hbm(array) for array in (right, first_moment, second_moment)))


def taken(array, places):
    count = places.shape[0]
    shape = (count, *array.shape[1:])

    def kernel(places, source, target):
        def one(b, carry):
            target[b] = source[places[b]]
            return carry

        lax.fori_loop(0, count, one, 0, unroll=4)

    here = pl.BlockSpec(memory_space=pltpu.VMEM)
    return pl.pallas_call(
        kernel,
        out_shape=jax.ShapeDtypeStruct(shape, array.dtype),
        in_specs=[pl.BlockSpec(memory_space=pltpu.SMEM), here],
        out_specs=here,
        compiler_params=pltpu.CompilerParams(vmem_limit_bytes=8 * mib),
        cost_estimate=pl.CostEstimate(
            flops=0,
            bytes_accessed=2 * array.size * array.dtype.itemsize,
            transcendentals=0,
        ),
    )(places, array)


def local(grad_parts, owner_table, left_basis, right_basis, first_moment, second_moment):
    replicas, halves, owners = (lax.axis_size(axis) for axis in ("dp", "half", "own"))
    _, block_count, piece_rows, width = grad_parts.shape
    quarter = width // replicas
    left = left_basis[0]

    parts = exchange(cut_columns(grad_parts[0], replicas), "dp")
    summed = parts.astype(jnp.float32).sum(axis=0).astype(jnp.bfloat16)

    slot_ids = slot_numbers(owner_table, owners)
    slot_range = jnp.arange(halves * owners, dtype=jnp.int32)
    selector = (slot_range[:, None] == slot_ids[None, :]).astype(jnp.bfloat16)
    packed = jnp.dot(
        selector,
        summed.reshape(block_count, piece_rows * quarter),
        preferred_element_type=jnp.float32,
    ).astype(jnp.bfloat16)
    block = exchange(packed.reshape(halves * owners, piece_rows, quarter), ("half", "own"))

    projected = exchange(
        projected_columns(block.reshape(width, quarter), left, replicas), "dp"
    )
    back = turned_step(projected, right_basis[0], first_moment[0], second_moment[0])
    back = exchange(back, "dp")
    update = jnp.dot(left, back.reshape(width, quarter), preferred_element_type=jnp.float32)

    outgoing = update.astype(jnp.bfloat16).reshape(halves * owners, piece_rows, quarter)
    returned = exchange(outgoing, ("half", "own"))
    return taken(returned, slot_ids)


def solution(mesh):
    slots = ("half", "own")
    return jax.shard_map(
        local,
        mesh=mesh,
        in_specs=(
            P("dp", None, slots, None),
            P(),
            P(slots, None, None),
            P(slots, None, None),
            P(slots, "dp", None),
            P(slots, "dp", None),
        ),
        out_specs=P(None, slots, "dp"),
        check_vma=False,
    )
```

time: 236 us -> 262 us (1.11)
  Pallas kernels: 2.97 us -> 40.2 us
  local copies, waits for them, and re-layouts: 8.95 us -> 2.02 us
  matrix products: 4.03 us -> 1.07 us
    pallas_call x1, Pallas kernels: 1.01 us -> 33.9 us  [cut_columns(): pl.pallas_call(kernel, out_shape=jax.ShapeDtypeStruct((pieces, blocks, ro...]
    unnamed x14 -> x6, local copies, waits for them, and re-layouts: 3.13 us -> 0.15 us
    dot_general x2 -> x0, matrix products: 2.96 us -> none  [the longest x1 2.65 us: local(): lax.dot_general(left, block.reshape(width, quarter), (((0,), (0,)), ((),...]
where the time goes in v3:
time: 262 us
  blocking collectives  203 us (77%)
  Pallas kernels  40.2 us (15%)
  waiting for transfers between devices  9.71 us (4%)
  starting transfers between devices  4.85 us (2%)
    all_to_all x4, blocking collectives, exchange(): return lax.all_to_all(array, axes, split_axis=0, concat_axis=0, tiled=True)  203 us
    pallas_call x1, Pallas kernels, cut_columns(): pl.pallas_call(kernel, out_shape=jax.ShapeDtypeStruct((pieces, blocks, ro...  33.9 us
    all_to_all x1, waiting for transfers between devices, exchange(): return lax.all_to_all(array, axes, split_axis=0, concat_axis=0, tiled=True)  9.71 us
  transfers between devices with their start and end apart: 1, of which 1 were waited for; matrix products, arithmetic and copies ran while one was open for 0% of the time, Pallas kernels for 0%

profile of v3, /device:TPU:1, one launch (start us, length us, event | category | flops | bytes accessed | tf_op | source)
XLA Modules:
  0.0 262.1 jit_solution(2751408113525649314)
XLA Ops:
  0.0 0.0 copy-start.1
  0.0 33.9 %shard_map.64 = bf16[4,132,4,256]{3,2,1,0:T(4,128)(2,1)} custom-call(bf16[132,4,1024]{2,1,0:T(4,128)(2,1)} %bitcast.20), custom_call_target="tpu_custom_call" | custom-call | bytes 2162688 | tf_op jit(solution)/shard_map/pallas_call | solution.py:48
  33.9 4.9 %all-to-all-start = ((bf16[4,132,4,256]{3,2,1,0:T(4,128)(2,1)}), bf16[4,132,4,256]{3,2,1,0:T(4,128)(2,1)S(1)}, u32[]{:S(2)}, u32[]{:S(2)}) async-start(bf16[4,132,4,256]{3,2,1,0:T(4,128)(2,1)} %shard_map.64), calls=%async_computation | async-start | bytes 2162688 | tf_op jit(solution)/shard_map/all_to_all | solution.py:21
  38.8 0.0 copy-done.1
  38.8 0.2 convert_reduce_fusion
  39.0 9.7 %all-to-all-done = bf16[4,132,4,256]{3,2,1,0:T(4,128)(2,1)S(1)} async-done(((bf16[4,132,4,256]{3,2,1,0:T(4,128)(2,1)}), bf16[4,132,4,256]{3,2,1,0:T(4,128)(2,1)S(1)}, u32[]{:S(2)}, u32[]{:S(2)}) %all-to-all-start) | async-done | bytes 1081376 | tf_op jit(solution)/shard_map/all_to_all | solution.py:21
  48.7 0.7 reduce_sum.22
  49.4 0.1 pad
  49.6 0.0 copy-start
  49.6 0.3 convolution_convert_fusion.1
  49.9 0.4 reshape.25
  50.3 106.3 %all_to_all.25 = bf16[256,4,256]{2,1,0:T(4,128)(2,1)} all-to-all(bf16[256,4,256]{2,1,0:T(4,128)(2,1)S(1)} %reshape.25), channel_id=1, replica_groups=mesh['dp'=4,'half'=4,'own'=64] {'half','own'}, dimensions={0} | all-to-all | bytes 1048576 | tf_op jit(solution)/shard_map/all_to_all | solution.py:21
  156.6 1.2 reshape.26.block
  157.7 0.0 copy-done
  157.7 0.8 shard_map.65
  158.5 10.5 %all_to_all.26.projected = bf16[4,256,256]{2,1,0:T(8,128)(2,1)S(1)} all-to-all(bf16[4,256,256]{2,1,0:T(8,128)(2,1)S(1)} %shard_map.65), channel_id=1, replica_groups=mesh['dp'=4,'half'=4,'own'=64] {'dp'}, dimensions={0} | all-to-all | bytes 1048576 | tf_op jit(solution)/shard_map/all_to_all | solution.py:21
  169.1 4.0 %shard_map.66 = bf16[4,256,256]{2,1,0:T(8,128)(2,1)S(1)} custom-call(bf16[4,256,256]{2,1,0:T(8,128)(2,1)S(1)} %all_to_all.26.projected, bf16[1024,1024]{1,0:T(8,128)(2,1)} %bitcast.17, bf16[256,1024]{1,0:T(8,128)(2,1)} %bitcast.22, bf16[256,1024]{1,0:T(8,128)(2,1)} %bitcast.23), custom_call_target="tpu_custom_call" | custom-call | flops 1073741824 | bytes 4194304 | tf_op jit(solution)/shard_map/pallas_call | solution.py:132
  173.1 11.6 %all_to_all.27 = bf16[4,256,256]{2,1,0:T(8,128)(2,1)S(1)} all-to-all(bf16[4,256,256]{2,1,0:T(8,128)(2,1)S(1)} %shard_map.66), channel_id=1, replica_groups=mesh['dp'=4,'half'=4,'own'=64] {'dp'}, dimensions={0} | all-to-all | bytes 1048576 | tf_op jit(solution)/shard_map/all_to_all | solution.py:21
  184.7 0.8 fusion
  185.5 0.2 copy.8
  185.7 0.1 reshape.28
  185.8 74.7 %all_to_all.28.source = bf16[256,4,256]{2,1,0:T(4,128)(2,1)S(1)} all-to-all(bf16[256,4,256]{2,1,0:T(4,128)(2,1)S(1)} %reshape.28), channel_id=1, replica_groups=mesh['dp'=4,'half'=4,'own'=64] {'half','own'}, dimensions={0} | all-to-all | bytes 1048576 | tf_op jit(solution)/shard_map/all_to_all | solution.py:21
  260.6 1.5 shard_map.67
  (2 shorter events, 0.0 us)
Async XLA Ops:
  0.0 38.8 %copy-start.1 = (s32[132,1]{0,1:T(1,128)S(1)}, s32[132,1]{0,1:T(1,128)}, u32[]{:S(2)}) copy-start(s32[132,1]{0,1:T(1,128)} %param.7) | copy-start | bytes 1588
  33.9 14.8 %all-to-all-start = ((bf16[4,132,4,256]{3,2,1,0:T(4,128)(2,1)}), bf16[4,132,4,256]{3,2,1,0:T(4,128)(2,1)S(1)}, u32[]{:S(2)}, u32[]{:S(2)}) async-start(bf16[4,132,4,256]{3,2,1,0:T(4,128)(2,1)} %shard_map.64), calls=%async_computation | async-start | bytes 2162688 | tf_op jit(solution)/shard_map/all_to_all | solution.py:21
  49.6 108.2 %copy-start = (bf16[1,1024,1024]{2,1,0:T(8,128)(2,1)S(1)}, bf16[1,1024,1024]{2,1,0:T(8,128)(2,1)}, u32[]{:S(2)}) copy-start(bf16[1,1024,1024]{2,1,0:T(8,128)(2,1)} %param.8) | copy-start | bytes 6291460

commit v4 on v3

--- a/solution.py
+++ b/solution.py
@@ -47,11 +47,11 @@
 
     return pl.pallas_call(
         kernel,
-        out_shape=jax.ShapeDtypeStruct((pieces, blocks, rows, part), array.dtype),
+        out_shape=pltpu.VMEM((pieces, blocks, rows, part), array.dtype),
         in_specs=[pl.BlockSpec(memory_space=pltpu.HBM)],
-        out_specs=pl.BlockSpec(memory_space=pltpu.HBM),
+        out_specs=pl.BlockSpec(memory_space=pltpu.VMEM),
         scratch_shapes=[pltpu.SemaphoreType.DMA((pieces,))],
-        compiler_params=pltpu.CompilerParams(vmem_limit_bytes=mib),
+        compiler_params=pltpu.CompilerParams(vmem_limit_bytes=8 * mib),
         cost_estimate=pl.CostEstimate(
             flops=0, bytes_accessed=2 * array.size * array.dtype.itemsize, transcendentals=0
         ),
@@ -87,34 +87,21 @@
     pieces, part, rows = projected.shape
     width = pieces * part
 
-    def kernel(projected, right, first, second, back, right_held, first_held, second_held, direction, done):
+    def kernel(projected, right, first, second, back, direction):
+        turned = projected[...].reshape(width, rows)
         cuts = [pl.ds(p * part, part) for p in range(pieces)]
-        pairs = ((right, right_held), (first, first_held), (second, second_held))
-        copies = [
-            [
-                pltpu.make_async_copy(source.at[:, cut], target.at[:, cut], done.at[n, p])
-                for n, (source, target) in enumerate(pairs)
-            ]
-            for p, cut in enumerate(cuts)
-        ]
-        for group in copies:
-            for copy in group:
-                copy.start()
-        turned = projected[...].reshape(width, rows)
-        for cut, group in zip(cuts, copies):
-            for copy in group:
-                copy.wait()
+        for cut in cuts:
             rotated = lax.dot_general(
                 turned,
-                right_held[:, cut],
+                right[:, cut],
                 (((0,), (0,)), ((), ())),
                 preferred_element_type=jnp.float32,
             )
             first_new = (
-                beta_first * first_held[:, cut].astype(jnp.float32) + (1.0 - beta_first) * rotated
+                beta_first * first[:, cut].astype(jnp.float32) + (1.0 - beta_first) * rotated
             )
             second_new = (
-                beta_second * second_held[:, cut].astype(jnp.float32)
+                beta_second * second[:, cut].astype(jnp.float32)
                 + (1.0 - beta_second) * rotated * rotated
             )
             direction[:, cut] = (
@@ -123,31 +110,42 @@
         for p, cut in enumerate(cuts):
             back[p] = lax.dot_general(
                 direction[...],
-                right_held[cut, :],
+                right[cut, :],
                 (((1,), (1,)), ((), ())),
                 preferred_element_type=jnp.float32,
             ).astype(jnp.bfloat16)
 
-    here, far = pl.BlockSpec(memory_space=pltpu.VMEM), pl.BlockSpec(memory_space=pltpu.HBM)
     return pl.pallas_call(
         kernel,
         out_shape=jax.ShapeDtypeStruct((pieces, rows, part), jnp.bfloat16),
-        in_specs=[here, far, far, far],
-        out_specs=here,
-        scratch_shapes=[
-            pltpu.VMEM((width, width), jnp.bfloat16),
-            pltpu.VMEM((rows, width), jnp.bfloat16),
-            pltpu.VMEM((rows, width), jnp.bfloat16),
-            pltpu.VMEM((rows, width), jnp.bfloat16),
-            pltpu.SemaphoreType.DMA((3, pieces)),
-        ],
+        scratch_shapes=[pltpu.VMEM((rows, width), jnp.bfloat16)],
         compiler_params=pltpu.CompilerParams(vmem_limit_bytes=16 * mib),
         cost_estimate=pl.CostEstimate(
             flops=4 * rows * width * width,
             bytes_accessed=2 * (width * width + 4 * rows * width),
             transcendentals=2 * rows * width,
         ),
-    )(projected, *(in_hbm(array) for array in (right, first_moment, second_moment)))
+    )(projected, right, first_moment, second_moment)
+
+
+def product(left, right):
+    def kernel(left, right, out):
+        out[...] = jnp.dot(
+            left[...], right[...], preferred_element_type=jnp.float32
+        ).astype(jnp.bfloat16)
+
+    rows, inner = left.shape
+    columns = right.shape[1]
+    return pl.pallas_call(
+        kernel,
+        out_shape=jax.ShapeDtypeStruct((rows, columns), jnp.bfloat16),
+        compiler_params=pltpu.CompilerParams(vmem_limit_bytes=16 * mib),
+        cost_estimate=pl.CostEstimate(
+            flops=2 * rows * inner * columns,
+            bytes_accessed=2 * (rows * inner + inner * columns + rows * columns),
+            transcendentals=0,
+        ),
+    )(left, right)
 
 
 def taken(array, places):
@@ -159,7 +157,7 @@
             target[b] = source[places[b]]
             return carry
 
-        lax.fori_loop(0, count, one, 0, unroll=4)
+        lax.fori_loop(0, count, one, 0, unroll=12)
 
     here = pl.BlockSpec(memory_space=pltpu.VMEM)
     return pl.pallas_call(
@@ -200,9 +198,9 @@
     )
     back = turned_step(projected, right_basis[0], first_moment[0], second_moment[0])
     back = exchange(back, "dp")
-    update = jnp.dot(left, back.reshape(width, quarter), preferred_element_type=jnp.float32)
-
-    outgoing = update.astype(jnp.bfloat16).reshape(halves * owners, piece_rows, quarter)
+    update = product(left, back.reshape(width, quarter))
+
+    outgoing = update.reshape(halves * owners, piece_rows, quarter)
     returned = exchange(outgoing, ("half", "own"))
     return taken(returned, slot_ids)
 

time: 262 us -> 228 us (0.87)
  Pallas kernels: 40.2 us -> 7.11 us
    pallas_call x1 -> x2, Pallas kernels: 33.9 us -> 2.94 us  [the longest x1 2.23 us: cut_columns(): pl.pallas_call(kernel, out_shape=pltpu.VMEM((pieces, blocks, rows, part),...]
where the time goes in v4:
time: 228 us; the launch traced here: 227 us
  blocking collectives  203 us (89%)
  waiting for transfers between devices  9.71 us (4%)
  Pallas kernels  7.11 us (3%)
  starting transfers between devices  4.85 us (2%)
    all_to_all x4, blocking collectives, exchange(): return lax.all_to_all(array, axes, split_axis=0, concat_axis=0, tiled=True)  203 us
    all_to_all x1, waiting for transfers between devices, exchange(): return lax.all_to_all(array, axes, split_axis=0, concat_axis=0, tiled=True)  9.71 us
    all_to_all x1, starting transfers between devices, exchange(): return lax.all_to_all(array, axes, split_axis=0, concat_axis=0, tiled=True)  4.85 us
  transfers between devices with their start and end apart: 1, of which 1 were waited for; matrix products, arithmetic and copies ran while one was open for 0% of the time, Pallas kernels for 0%

profile of v4, /device:TPU:1, one launch (start us, length us, event | category | flops | bytes accessed | tf_op | source)
XLA Modules:
  0.0 227.2 jit_solution(3400638574301217498)
XLA Ops:
  0.0 2.2 shard_map.64
  2.2 0.0 copy-start.4
  2.3 4.9 %all-to-all-start = ((bf16[4,132,4,256]{3,2,1,0:T(4,128)(2,1)}), bf16[4,132,4,256]{3,2,1,0:T(4,128)(2,1)S(1)}, u32[]{:S(2)}, u32[]{:S(2)}) async-start(bf16[4,132,4,256]{3,2,1,0:T(4,128)(2,1)} %shard_map.64), calls=%async_computation | async-start | bytes 2162688 | tf_op jit(solution)/shard_map/all_to_all | solution.py:21
  7.1 0.0 copy-done.4
  7.1 0.2 convert_reduce_fusion
  7.3 9.7 %all-to-all-done = bf16[4,132,4,256]{3,2,1,0:T(4,128)(2,1)S(1)} async-done(((bf16[4,132,4,256]{3,2,1,0:T(4,128)(2,1)}), bf16[4,132,4,256]{3,2,1,0:T(4,128)(2,1)S(1)}, u32[]{:S(2)}, u32[]{:S(2)}) %all-to-all-start) | async-done | bytes 1081376 | tf_op jit(solution)/shard_map/all_to_all | solution.py:21
  17.0 0.7 reduce_sum.22
  17.7 0.1 pad
  17.9 0.3 convolution_convert_fusion
  18.2 0.4 reshape.25
  18.6 0.0 copy-start
  18.6 106.3 %all_to_all.25 = bf16[256,4,256]{2,1,0:T(4,128)(2,1)S(1)} all-to-all(bf16[256,4,256]{2,1,0:T(4,128)(2,1)S(1)} %reshape.25), channel_id=1, replica_groups=mesh['dp'=4,'half'=4,'own'=64] {'half','own'}, dimensions={0} | all-to-all | bytes 1048576 | tf_op jit(solution)/shard_map/all_to_all | solution.py:21
  124.9 0.1 reshape.26.block
  125.1 0.0 copy-start.1
  125.1 0.8 shard_map.65
  125.8 0.0 copy-start.2
  125.8 0.0 copy-start.3
  125.9 10.7 %all_to_all.26.projected = bf16[4,256,256]{2,1,0:T(8,128)(2,1)S(1)} all-to-all(bf16[4,256,256]{2,1,0:T(8,128)(2,1)S(1)} %shard_map.65), channel_id=1, replica_groups=mesh['dp'=4,'half'=4,'own'=64] {'dp'}, dimensions={0} | all-to-all | bytes 1048576 | tf_op jit(solution)/shard_map/all_to_all | solution.py:21
  136.5 2.0 shard_map.66
  138.5 11.7 %all_to_all.27 = bf16[4,256,256]{2,1,0:T(8,128)(2,1)S(1)} all-to-all(bf16[4,256,256]{2,1,0:T(8,128)(2,1)S(1)} %shard_map.66), channel_id=1, replica_groups=mesh['dp'=4,'half'=4,'own'=64] {'dp'}, dimensions={0} | all-to-all | bytes 1048576 | tf_op jit(solution)/shard_map/all_to_all | solution.py:21
  150.2 0.7 shard_map.67
  150.9 0.1 reshape.28
  151.0 74.7 %all_to_all.28.source = bf16[256,4,256]{2,1,0:T(4,128)(2,1)S(1)} all-to-all(bf16[256,4,256]{2,1,0:T(4,128)(2,1)S(1)} %reshape.28), channel_id=1, replica_groups=mesh['dp'=4,'half'=4,'own'=64] {'half','own'}, dimensions={0} | all-to-all | bytes 1048576 | tf_op jit(solution)/shard_map/all_to_all | solution.py:21
  225.8 1.4 shard_map.68
  (6 shorter events, 0.0 us)
Async XLA Ops:
  2.2 4.9 %copy-start.4 = (s32[132,1]{0,1:T(1,128)S(1)}, s32[132,1]{0,1:T(1,128)}, u32[]{:S(2)}) copy-start(s32[132,1]{0,1:T(1,128)} %param.7) | copy-start | bytes 1588
  2.3 14.8 %all-to-all-start = ((bf16[4,132,4,256]{3,2,1,0:T(4,128)(2,1)}), bf16[4,132,4,256]{3,2,1,0:T(4,128)(2,1)S(1)}, u32[]{:S(2)}, u32[]{:S(2)}) async-start(bf16[4,132,4,256]{3,2,1,0:T(4,128)(2,1)} %shard_map.64), calls=%async_computation | async-start | bytes 2162688 | tf_op jit(solution)/shard_map/all_to_all | solution.py:21
  18.6 106.5 %copy-start = (bf16[1,1024,1024]{2,1,0:T(8,128)(2,1)S(1)}, bf16[1,1024,1024]{2,1,0:T(8,128)(2,1)}, u32[]{:S(2)}) copy-start(bf16[1,1024,1024]{2,1,0:T(8,128)(2,1)} %param.8) | copy-start | bytes 6291460
  125.1 11.5 %copy-start.1 = (bf16[1,1024,1024]{2,1,0:T(8,128)(2,1)S(1)}, bf16[1,1024,1024]{2,1,0:T(8,128)(2,1)}, u32[]{:S(2)}) copy-start(bf16[1,1024,1024]{2,1,0:T(8,128)(2,1)} %param.9) | copy-start | bytes 6291460
  125.8 10.7 %copy-start.2 = (bf16[1,256,1024]{2,1,0:T(8,128)(2,1)S(1)}, bf16[1,256,1024]{2,1,0:T(8,128)(2,1)}, u32[]{:S(2)}) copy-start(bf16[1,256,1024]{2,1,0:T(8,128)(2,1)} %param.10) | copy-start | bytes 1572868
  125.8 10.7 %copy-start.3 = (bf16[1,256,1024]{2,1,0:T(8,128)(2,1)S(1)}, bf16[1,256,1024]{2,1,0:T(8,128)(2,1)}, u32[]{:S(2)}) copy-start(bf16[1,256,1024]{2,1,0:T(8,128)(2,1)} %param.11) | copy-start | bytes 1572868

commit v5 on v4

--- a/solution.py
+++ b/solution.py
@@ -3,7 +3,7 @@
 from jax import lax
 from jax.experimental import pallas as pl
 from jax.experimental.pallas import tpu as pltpu
-from jax.sharding import PartitionSpec as P
+from jax.sharding import Mesh, PartitionSpec as P
 
 beta_first = 0.9
 beta_second = 0.95
@@ -11,6 +11,7 @@
 bias_second = 1.0 - 0.95**10
 epsilon = 1e-08
 mib = 1 << 20
+cores = 2
 
 
 def in_hbm(array):
@@ -21,12 +22,19 @@
     return lax.all_to_all(array, axes, split_axis=0, concat_axis=0, tiled=True)
 
 
-def slot_numbers(owner_table, owner_count):
+def slot_places(owner_table, ranks, depth):
     owner_ids = owner_table[:, 0]
     positions = jnp.arange(owner_ids.shape[0], dtype=jnp.int32)
     shared = (owner_ids[:, None] == owner_ids[None, :]) & (positions[None, :] < positions[:, None])
     ranking = jnp.sum(shared.astype(jnp.int32), axis=1)
-    return ranking * owner_count + owner_ids
+    return ((owner_ids % cores) * ranks + ranking) * depth + owner_ids // cores
+
+
+def in_turn(array, depth):
+    away = depth * 3 // 8
+    pairs = [(z * cores + 1, (z + away) % depth * cores + 1) for z in range(depth)]
+    turn = lax.ppermute(array[0, 0], ("z", "core"), pairs)
+    return lax.optimization_barrier((array, turn))
 
 
 def cut_columns(array, pieces):
@@ -58,11 +66,11 @@
     )(in_hbm(array))
 
 
-def projected_columns(block, left, pieces):
+def projected_columns(block, left, pieces, after):
     width, columns = block.shape
     part = width // pieces
 
-    def kernel(block, left, out):
+    def kernel(block, left, after, out):
         for p in range(pieces):
             out[p] = lax.dot_general(
                 block[...],
@@ -74,13 +82,14 @@
     return pl.pallas_call(
         kernel,
         out_shape=jax.ShapeDtypeStruct((pieces, columns, part), jnp.bfloat16),
+        in_specs=[pl.BlockSpec(memory_space=space) for space in (pltpu.VMEM, pltpu.VMEM, pl.ANY)],
         compiler_params=pltpu.CompilerParams(vmem_limit_bytes=16 * mib),
         cost_estimate=pl.CostEstimate(
             flops=2 * width * width * columns,
             bytes_accessed=2 * (width * width + 2 * width * columns),
             transcendentals=0,
         ),
-    )(block, left)
+    )(block, left, after)
 
 
 def turned_step(projected, right, first_moment, second_moment):
@@ -175,7 +184,8 @@
 
 
 def local(grad_parts, owner_table, left_basis, right_basis, first_moment, second_moment):
-    replicas, halves, owners = (lax.axis_size(axis) for axis in ("dp", "half", "own"))
+    replicas, halves, depth = (lax.axis_size(axis) for axis in ("dp", "half", "z"))
+    slots = halves * depth
     _, block_count, piece_rows, width = grad_parts.shape
     quarter = width // replicas
     left = left_basis[0]
@@ -183,33 +193,40 @@
     parts = exchange(cut_columns(grad_parts[0], replicas), "dp")
     summed = parts.astype(jnp.float32).sum(axis=0).astype(jnp.bfloat16)
 
-    slot_ids = slot_numbers(owner_table, owners)
-    slot_range = jnp.arange(halves * owners, dtype=jnp.int32)
-    selector = (slot_range[:, None] == slot_ids[None, :]).astype(jnp.bfloat16)
+    places = slot_places(owner_table, halves, depth)
+    selector = (jnp.arange(cores * slots, dtype=jnp.int32)[:, None] == places[None, :]).astype(
+        jnp.bfloat16
+    )
     packed = jnp.dot(
         selector,
         summed.reshape(block_count, piece_rows * quarter),
         preferred_element_type=jnp.float32,
     ).astype(jnp.bfloat16)
-    block = exchange(packed.reshape(halves * owners, piece_rows, quarter), ("half", "own"))
+    arrived = exchange(packed.reshape(cores, slots, piece_rows, quarter), "core")
+    arrived, turn = in_turn(jnp.moveaxis(arrived, 1, 0), depth)
+    block = exchange(arrived, ("half", "z"))
 
     projected = exchange(
-        projected_columns(block.reshape(width, quarter), left, replicas), "dp"
+        projected_columns(block.reshape(width, quarter), left, replicas, turn), "dp"
     )
     back = turned_step(projected, right_basis[0], first_moment[0], second_moment[0])
     back = exchange(back, "dp")
     update = product(left, back.reshape(width, quarter))
 
-    outgoing = update.reshape(halves * owners, piece_rows, quarter)
-    returned = exchange(outgoing, ("half", "own"))
-    return taken(returned, slot_ids)
+    returned = exchange(update.reshape(slots, cores, piece_rows, quarter), ("half", "z"))
+    returned = exchange(jnp.moveaxis(returned, 1, 0), "core")
+    return taken(returned.reshape(cores * slots, piece_rows, quarter), places)
 
 
 def solution(mesh):
-    slots = ("half", "own")
+    replicas, halves, owners = (mesh.shape[axis] for axis in ("dp", "half", "own"))
+    fine = Mesh(
+        mesh.devices.reshape(replicas, halves, owners // cores, cores), ("dp", "half", "z", "core")
+    )
+    slots = ("half", "z", "core")
     return jax.shard_map(
         local,
-        mesh=mesh,
+        mesh=fine,
         in_specs=(
             P("dp", None, slots, None),
             P(),

time: 228 us -> 222 us (0.974)
  blocking collectives: 203 us -> 178 us
  starting transfers between devices: 4.85 us -> 19.6 us
  waiting for transfers between devices: 9.71 us -> 14.3 us
    all_to_all x4 -> x6, blocking collectives: 203 us -> 178 us  [exchange(): return lax.all_to_all(array, axes, split_axis=0, concat_axis=0, tiled=True)]
    ppermute x0 -> x1, starting transfers between devices: none -> 14.7 us  [in_turn(): turn = lax.ppermute(array[0, 0], ('z', 'core'), pairs)]
    ppermute x0 -> x1, waiting for transfers between devices: none -> 4.6 us  [in_turn(): turn = lax.ppermute(array[0, 0], ('z', 'core'), pairs)]
  transfers between devices with their start and end apart: 1 -> 2, of which waited for: 1 -> 2; matrix products, arithmetic and copies ran while one was open for 0% -> 0% of each run, Pallas kernels for 0% -> 0%
where the time goes in v5:
time: 222 us; the launch traced here: 221 us
  blocking collectives  178 us (80%)
  starting transfers between devices  19.6 us (9%)
  waiting for transfers between devices  14.3 us (6%)
  Pallas kernels  7.12 us (3%)
    all_to_all x6, blocking collectives, exchange(): return lax.all_to_all(array, axes, split_axis=0, concat_axis=0, tiled=True)  178 us
    ppermute x1, starting transfers between devices, in_turn(): turn = lax.ppermute(array[0, 0], ('z', 'core'), pairs)  14.7 us
    all_to_all x1, waiting for transfers between devices, exchange(): return lax.all_to_all(array, axes, split_axis=0, concat_axis=0, tiled=True)  9.7 us
    all_to_all x1, starting transfers between devices, exchange(): return lax.all_to_all(array, axes, split_axis=0, concat_axis=0, tiled=True)  4.85 us
    ppermute x1, waiting for transfers between devices, in_turn(): turn = lax.ppermute(array[0, 0], ('z', 'core'), pairs)  4.6 us
  transfers between devices with their start and end apart: 2, of which 2 were waited for; matrix products, arithmetic and copies ran while one was open for 0% of the time, Pallas kernels for 0%

profile of v5, /device:TPU:1, one launch (start us, length us, event | category | flops | bytes accessed | tf_op | source)
XLA Modules:
  0.0 221.4 jit_solution(15496836149736312633)
XLA Ops:
  0.0 2.2 %shard_map.64 = bf16[4,132,4,256]{3,2,1,0:T(4,128)(2,1)} custom-call(bf16[132,4,1024]{2,1,0:T(4,128)(2,1)} %bitcast.30), custom_call_target="tpu_custom_call" | custom-call | bytes 2162688 | tf_op jit(solution)/shard_map/pallas_call | solution.py:56
  2.2 4.9 %all-to-all-start = ((bf16[4,132,4,256]{3,2,1,0:T(4,128)(2,1)}), bf16[4,132,4,256]{3,2,1,0:T(4,128)(2,1)S(1)}, u32[]{:S(2)}, u32[]{:S(2)}) async-start(bf16[4,132,4,256]{3,2,1,0:T(4,128)(2,1)} %shard_map.64), calls=%async_computation | async-start | bytes 2162688 | tf_op jit(solution)/shard_map/all_to_all | solution.py:22
  7.1 0.2 convert_reduce_fusion
  7.3 9.7 %all-to-all-done = bf16[4,132,4,256]{3,2,1,0:T(4,128)(2,1)S(1)} async-done(((bf16[4,132,4,256]{3,2,1,0:T(4,128)(2,1)}), bf16[4,132,4,256]{3,2,1,0:T(4,128)(2,1)S(1)}, u32[]{:S(2)}, u32[]{:S(2)}) %all-to-all-start) | async-done | bytes 1081376 | tf_op jit(solution)/shard_map/all_to_all | solution.py:22
  17.0 0.7 reduce_sum.22
  17.7 0.1 pad
  17.9 0.3 convolution_convert_fusion
  18.2 0.4 reshape.74
  18.6 17.7 %all_to_all.35 = bf16[2,128,4,256]{3,2,1,0:T(4,128)(2,1)S(1)} all-to-all(bf16[2,128,4,256]{3,2,1,0:T(4,128)(2,1)S(1)} %reshape.74), channel_id=1, replica_groups=mesh['dp'=4,'half'=4,'z'=32,'core'=2] {'core'}, dimensions={0} | all-to-all | bytes 1048576 | tf_op jit(solution)/shard_map/all_to_all | solution.py:22
  36.3 0.2 copy.18
  36.5 14.7 %collective-permute-start = (bf16[4,256]{1,0:T(4,128)(2,1)S(1)}, bf16[4,256]{1,0:T(4,128)(2,1)S(1)}, u32[]{:S(2)}, u32[]{:S(2)}) collective-permute-start(bf16[4,256]{1,0:T(4,128)(2,1)S(1)} %slice_bitcast_fusion), channel_id=1, source_target_pairs={{1,25},{3,27},{5,29},{7,31},{9,33},{11,35},{13,37},{15,39},{17,41}... | collective-permute-start | bytes 6152 | tf_op jit(solution)/shard_map/ppermute | solution.py:36
  51.2 4.6 %collective-permute-done.after = bf16[4,256]{1,0:T(4,128)(2,1)S(1)} collective-permute-done((bf16[4,256]{1,0:T(4,128)(2,1)S(1)}, bf16[4,256]{1,0:T(4,128)(2,1)S(1)}, u32[]{:S(2)}, u32[]{:S(2)}) %collective-permute-start) | collective-permute-done | bytes 2080 | tf_op jit(solution)/shard_map/ppermute | solution.py:36
  55.8 73.2 %all_to_all.36 = bf16[128,2,4,256]{3,2,1,0:T(4,128)(2,1)S(1)} all-to-all(bf16[128,2,4,256]{3,2,1,0:T(4,128)(2,1)S(1)} %bitcast.26), channel_id=1, replica_groups=mesh['dp'=4,'half'=4,'z'=32,'core'=2] {'half','z'}, dimensions={0} | all-to-all | bytes 1048576 | tf_op jit(solution)/shard_map/all_to_all | solution.py:22
  129.0 0.1 reshape.75.block
  129.2 0.8 shard_map.65
  130.0 9.5 %all_to_all.37.projected = bf16[4,256,256]{2,1,0:T(8,128)(2,1)S(1)} all-to-all(bf16[4,256,256]{2,1,0:T(8,128)(2,1)S(1)} %shard_map.65), channel_id=1, replica_groups=mesh['dp'=4,'half'=4,'z'=32,'core'=2] {'dp'}, dimensions={0} | all-to-all | bytes 1048576 | tf_op jit(solution)/shard_map/all_to_all | solution.py:22
  139.4 2.0 shard_map.66
  141.4 9.3 %all_to_all.38 = bf16[4,256,256]{2,1,0:T(8,128)(2,1)S(1)} all-to-all(bf16[4,256,256]{2,1,0:T(8,128)(2,1)S(1)} %shard_map.66), channel_id=1, replica_groups=mesh['dp'=4,'half'=4,'z'=32,'core'=2] {'dp'}, dimensions={0} | all-to-all | bytes 1048576 | tf_op jit(solution)/shard_map/all_to_all | solution.py:22
  150.8 0.7 shard_map.67
  151.5 0.1 reshape.77
  151.6 64.4 %all_to_all.39 = bf16[128,2,4,256]{3,2,1,0:T(4,128)(2,1)S(1)} all-to-all(bf16[128,2,4,256]{3,2,1,0:T(4,128)(2,1)S(1)} %reshape.77), channel_id=1, replica_groups=mesh['dp'=4,'half'=4,'z'=32,'core'=2] {'half','z'}, dimensions={0} | all-to-all | bytes 1048576 | tf_op jit(solution)/shard_map/all_to_all | solution.py:22
  216.0 0.2 copy.15
  216.2 3.8 %all_to_all.40 = bf16[2,128,4,256]{3,2,1,0:T(4,128)(2,1)S(1)} all-to-all(bf16[2,128,4,256]{3,2,1,0:T(4,128)(2,1)S(1)} %copy.15), channel_id=1, replica_groups=mesh['dp'=4,'half'=4,'z'=32,'core'=2] {'core'}, dimensions={0} | all-to-all | bytes 1048576 | tf_op jit(solution)/shard_map/all_to_all | solution.py:22
  220.0 1.4 shard_map.68
  (13 shorter events, 0.1 us)
Async XLA Ops:
  2.2 4.9 %copy-start.4 = (s32[132,1]{0,1:T(1,128)S(1)}, s32[132,1]{0,1:T(1,128)}, u32[]{:S(2)}) copy-start(s32[132,1]{0,1:T(1,128)} %param.7) | copy-start | bytes 1588
  2.2 14.8 %all-to-all-start = ((bf16[4,132,4,256]{3,2,1,0:T(4,128)(2,1)}), bf16[4,132,4,256]{3,2,1,0:T(4,128)(2,1)S(1)}, u32[]{:S(2)}, u32[]{:S(2)}) async-start(bf16[4,132,4,256]{3,2,1,0:T(4,128)(2,1)} %shard_map.64), calls=%async_computation | async-start | bytes 2162688 | tf_op jit(solution)/shard_map/all_to_all | solution.py:22
  36.5 92.7 %copy-start = (bf16[1,1024,1024]{2,1,0:T(8,128)(2,1)S(1)}, bf16[1,1024,1024]{2,1,0:T(8,128)(2,1)}, u32[]{:S(2)}) copy-start(bf16[1,1024,1024]{2,1,0:T(8,128)(2,1)} %param.8) | copy-start | bytes 6291460
  36.5 19.3 %collective-permute-start = (bf16[4,256]{1,0:T(4,128)(2,1)S(1)}, bf16[4,256]{1,0:T(4,128)(2,1)S(1)}, u32[]{:S(2)}, u32[]{:S(2)}) collective-permute-start(bf16[4,256]{1,0:T(4,128)(2,1)S(1)} %slice_bitcast_fusion), channel_id=1, source_target_pairs={{1,25},{3,27},{5,29},{7,31},{9,33},{11,35},{13,37},{15,39},{17,41}... | collective-permute-start | bytes 6152 | tf_op jit(solution)/shard_map/ppermute | solution.py:36
  129.1 10.3 %copy-start.1 = (bf16[1,1024,1024]{2,1,0:T(8,128)(2,1)S(1)}, bf16[1,1024,1024]{2,1,0:T(8,128)(2,1)}, u32[]{:S(2)}) copy-start(bf16[1,1024,1024]{2,1,0:T(8,128)(2,1)} %param.9) | copy-start | bytes 6291460
  129.9 9.5 %copy-start.2 = (bf16[1,256,1024]{2,1,0:T(8,128)(2,1)S(1)}, bf16[1,256,1024]{2,1,0:T(8,128)(2,1)}, u32[]{:S(2)}) copy-start(bf16[1,256,1024]{2,1,0:T(8,128)(2,1)} %param.10) | copy-start | bytes 1572868
  129.9 9.5 %copy-start.3 = (bf16[1,256,1024]{2,1,0:T(8,128)(2,1)S(1)}, bf16[1,256,1024]{2,1,0:T(8,128)(2,1)}, u32[]{:S(2)}) copy-start(bf16[1,256,1024]{2,1,0:T(8,128)(2,1)} %param.11) | copy-start | bytes 1572868

commit v6 on v5

--- a/solution.py
+++ b/solution.py
@@ -31,7 +31,7 @@
 
 
 def in_turn(array, depth):
-    away = depth * 3 // 8
+    away = depth // 2
     pairs = [(z * cores + 1, (z + away) % depth * cores + 1) for z in range(depth)]
     turn = lax.ppermute(array[0, 0], ("z", "core"), pairs)
     return lax.optimization_barrier((array, turn))
@@ -161,12 +161,17 @@
     count = places.shape[0]
     shape = (count, *array.shape[1:])
 
+    batch = max(n for n in range(1, 13) if count % n == 0)
+
     def kernel(places, source, target):
-        def one(b, carry):
-            target[b] = source[places[b]]
+        def some(step, carry):
+            first = step * batch
+            rows = [source[places[first + n]] for n in range(batch)]
+            for n, row in enumerate(rows):
+                target[first + n] = row
             return carry
 
-        lax.fori_loop(0, count, one, 0, unroll=12)
+        lax.fori_loop(0, count // batch, some, 0)
 
     here = pl.BlockSpec(memory_space=pltpu.VMEM)
     return pl.pallas_call(

time: 222 us -> 213 us (0.959)
  blocking collectives: 178 us -> 166 us
  starting transfers between devices: 19.6 us -> 26.2 us
  waiting for transfers between devices: 14.3 us -> 11.1 us
    all_to_all x6, blocking collectives: 178 us -> 166 us  [exchange(): return lax.all_to_all(array, axes, split_axis=0, concat_axis=0, tiled=True)]
    ppermute x1, starting transfers between devices: 14.7 us -> 21.4 us  [in_turn(): turn = lax.ppermute(array[0, 0], ('z', 'core'), pairs)]
    ppermute x1, waiting for transfers between devices: 4.6 us -> 1.42 us  [in_turn(): turn = lax.ppermute(array[0, 0], ('z', 'core'), pairs)]
where the time goes in v6:
time: 213 us
  blocking collectives  166 us (78%)
  starting transfers between devices  26.2 us (12%)
  waiting for transfers between devices  11.1 us (5%)
  Pallas kernels  7.13 us (3%)
    all_to_all x6, blocking collectives, exchange(): return lax.all_to_all(array, axes, split_axis=0, concat_axis=0, tiled=True)  166 us
    ppermute x1, starting transfers between devices, in_turn(): turn = lax.ppermute(array[0, 0], ('z', 'core'), pairs)  21.4 us
    all_to_all x1, waiting for transfers between devices, exchange(): return lax.all_to_all(array, axes, split_axis=0, concat_axis=0, tiled=True)  9.7 us
    all_to_all x1, starting transfers between devices, exchange(): return lax.all_to_all(array, axes, split_axis=0, concat_axis=0, tiled=True)  4.85 us
  transfers between devices with their start and end apart: 2, of which 2 were waited for; matrix products, arithmetic and copies ran while one was open for 0% of the time, Pallas kernels for 0%

profile of v6, /device:TPU:1, one launch (start us, length us, event | category | flops | bytes accessed | tf_op | source)
XLA Modules:
  0.0 213.1 jit_solution(4475026333350121995)
XLA Ops:
  0.0 2.2 %shard_map.64 = bf16[4,132,4,256]{3,2,1,0:T(4,128)(2,1)} custom-call(bf16[132,4,1024]{2,1,0:T(4,128)(2,1)} %bitcast.30), custom_call_target="tpu_custom_call" | custom-call | bytes 2162688 | tf_op jit(solution)/shard_map/pallas_call | solution.py:56
  2.2 4.9 %all-to-all-start = ((bf16[4,132,4,256]{3,2,1,0:T(4,128)(2,1)}), bf16[4,132,4,256]{3,2,1,0:T(4,128)(2,1)S(1)}, u32[]{:S(2)}, u32[]{:S(2)}) async-start(bf16[4,132,4,256]{3,2,1,0:T(4,128)(2,1)} %shard_map.64), calls=%async_computation | async-start | bytes 2162688 | tf_op jit(solution)/shard_map/all_to_all | solution.py:22
  7.1 0.2 convert_reduce_fusion
  7.3 9.7 %all-to-all-done = bf16[4,132,4,256]{3,2,1,0:T(4,128)(2,1)S(1)} async-done(((bf16[4,132,4,256]{3,2,1,0:T(4,128)(2,1)}), bf16[4,132,4,256]{3,2,1,0:T(4,128)(2,1)S(1)}, u32[]{:S(2)}, u32[]{:S(2)}) %all-to-all-start) | async-done | bytes 1081376 | tf_op jit(solution)/shard_map/all_to_all | solution.py:22
  17.0 0.7 reduce_sum.22
  17.7 0.1 pad
  17.9 0.3 convolution_convert_fusion
  18.2 0.4 reshape.74
  18.6 17.7 %all_to_all.35 = bf16[2,128,4,256]{3,2,1,0:T(4,128)(2,1)S(1)} all-to-all(bf16[2,128,4,256]{3,2,1,0:T(4,128)(2,1)S(1)} %reshape.74), channel_id=1, replica_groups=mesh['dp'=4,'half'=4,'z'=32,'core'=2] {'core'}, dimensions={0} | all-to-all | bytes 1048576 | tf_op jit(solution)/shard_map/all_to_all | solution.py:22
  36.3 0.2 copy.18
  36.5 21.4 %collective-permute-start = (bf16[4,256]{1,0:T(4,128)(2,1)S(1)}, bf16[4,256]{1,0:T(4,128)(2,1)S(1)}, u32[]{:S(2)}, u32[]{:S(2)}) collective-permute-start(bf16[4,256]{1,0:T(4,128)(2,1)S(1)} %slice_bitcast_fusion), channel_id=1, source_target_pairs={{1,33},{3,35},{5,37},{7,39},{9,41},{11,43},{13,45},{15,47},{17,49}... | collective-permute-start | bytes 6152 | tf_op jit(solution)/shard_map/ppermute | solution.py:36
  57.9 1.4 collective-permute-done.after
  59.3 69.4 %all_to_all.36 = bf16[128,2,4,256]{3,2,1,0:T(4,128)(2,1)S(1)} all-to-all(bf16[128,2,4,256]{3,2,1,0:T(4,128)(2,1)S(1)} %bitcast.26), channel_id=1, replica_groups=mesh['dp'=4,'half'=4,'z'=32,'core'=2] {'half','z'}, dimensions={0} | all-to-all | bytes 1048576 | tf_op jit(solution)/shard_map/all_to_all | solution.py:22
  128.7 0.1 reshape.75.block
  128.9 0.8 shard_map.65
  129.7 9.5 %all_to_all.37.projected = bf16[4,256,256]{2,1,0:T(8,128)(2,1)S(1)} all-to-all(bf16[4,256,256]{2,1,0:T(8,128)(2,1)S(1)} %shard_map.65), channel_id=1, replica_groups=mesh['dp'=4,'half'=4,'z'=32,'core'=2] {'dp'}, dimensions={0} | all-to-all | bytes 1048576 | tf_op jit(solution)/shard_map/all_to_all | solution.py:22
  139.1 2.0 shard_map.66
  141.1 9.6 %all_to_all.38 = bf16[4,256,256]{2,1,0:T(8,128)(2,1)S(1)} all-to-all(bf16[4,256,256]{2,1,0:T(8,128)(2,1)S(1)} %shard_map.66), channel_id=1, replica_groups=mesh['dp'=4,'half'=4,'z'=32,'core'=2] {'dp'}, dimensions={0} | all-to-all | bytes 1048576 | tf_op jit(solution)/shard_map/all_to_all | solution.py:22
  150.8 0.7 shard_map.67
  151.5 0.1 reshape.77
  151.6 56.0 %all_to_all.39 = bf16[128,2,4,256]{3,2,1,0:T(4,128)(2,1)S(1)} all-to-all(bf16[128,2,4,256]{3,2,1,0:T(4,128)(2,1)S(1)} %reshape.77), channel_id=1, replica_groups=mesh['dp'=4,'half'=4,'z'=32,'core'=2] {'half','z'}, dimensions={0} | all-to-all | bytes 1048576 | tf_op jit(solution)/shard_map/all_to_all | solution.py:22
  207.6 0.2 copy.15
  207.8 3.8 %all_to_all.40 = bf16[2,128,4,256]{3,2,1,0:T(4,128)(2,1)S(1)} all-to-all(bf16[2,128,4,256]{3,2,1,0:T(4,128)(2,1)S(1)} %copy.15), channel_id=1, replica_groups=mesh['dp'=4,'half'=4,'z'=32,'core'=2] {'core'}, dimensions={0} | all-to-all | bytes 1048576 | tf_op jit(solution)/shard_map/all_to_all | solution.py:22
  211.6 1.4 shard_map.68
  (13 shorter events, 0.1 us)
Async XLA Ops:
  2.2 4.9 %copy-start.4 = (s32[132,1]{0,1:T(1,128)S(1)}, s32[132,1]{0,1:T(1,128)}, u32[]{:S(2)}) copy-start(s32[132,1]{0,1:T(1,128)} %param.7) | copy-start | bytes 1588
  2.2 14.8 %all-to-all-start = ((bf16[4,132,4,256]{3,2,1,0:T(4,128)(2,1)}), bf16[4,132,4,256]{3,2,1,0:T(4,128)(2,1)S(1)}, u32[]{:S(2)}, u32[]{:S(2)}) async-start(bf16[4,132,4,256]{3,2,1,0:T(4,128)(2,1)} %shard_map.64), calls=%async_computation | async-start | bytes 2162688 | tf_op jit(solution)/shard_map/all_to_all | solution.py:22
  36.5 92.4 %copy-start = (bf16[1,1024,1024]{2,1,0:T(8,128)(2,1)S(1)}, bf16[1,1024,1024]{2,1,0:T(8,128)(2,1)}, u32[]{:S(2)}) copy-start(bf16[1,1024,1024]{2,1,0:T(8,128)(2,1)} %param.8) | copy-start | bytes 6291460
  36.5 22.8 %collective-permute-start = (bf16[4,256]{1,0:T(4,128)(2,1)S(1)}, bf16[4,256]{1,0:T(4,128)(2,1)S(1)}, u32[]{:S(2)}, u32[]{:S(2)}) collective-permute-start(bf16[4,256]{1,0:T(4,128)(2,1)S(1)} %slice_bitcast_fusion), channel_id=1, source_target_pairs={{1,33},{3,35},{5,37},{7,39},{9,41},{11,43},{13,45},{15,47},{17,49}... | collective-permute-start | bytes 6152 | tf_op jit(solution)/shard_map/ppermute | solution.py:36
  128.9 10.3 %copy-start.1 = (bf16[1,1024,1024]{2,1,0:T(8,128)(2,1)S(1)}, bf16[1,1024,1024]{2,1,0:T(8,128)(2,1)}, u32[]{:S(2)}) copy-start(bf16[1,1024,1024]{2,1,0:T(8,128)(2,1)} %param.9) | copy-start | bytes 6291460
  129.6 9.5 %copy-start.2 = (bf16[1,256,1024]{2,1,0:T(8,128)(2,1)S(1)}, bf16[1,256,1024]{2,1,0:T(8,128)(2,1)}, u32[]{:S(2)}) copy-start(bf16[1,256,1024]{2,1,0:T(8,128)(2,1)} %param.10) | copy-start | bytes 1572868
  129.6 9.5 %copy-start.3 = (bf16[1,256,1024]{2,1,0:T(8,128)(2,1)S(1)}, bf16[1,256,1024]{2,1,0:T(8,128)(2,1)}, u32[]{:S(2)}) copy-start(bf16[1,256,1024]{2,1,0:T(8,128)(2,1)} %param.11) | copy-start | bytes 1572868

commit v7 on v6

--- a/solution.py
+++ b/solution.py
@@ -41,24 +41,42 @@
     blocks, rows, width = array.shape
     part = width // pieces
 
-    def kernel(source, target, done):
-        copies = [
-            pltpu.make_async_copy(
-                source.at[:, :, pl.ds(p * part, part)], target.at[p], done.at[p]
-            )
-            for p in range(pieces)
-        ]
-        for copy in copies:
-            copy.start()
-        for copy in copies:
-            copy.wait()
-
-    return pl.pallas_call(
-        kernel,
-        out_shape=pltpu.VMEM((pieces, blocks, rows, part), array.dtype),
+    steps = max(n for n in range(1, 5) if blocks % n == 0)
+    some = blocks // steps
+
+    def kernel(source, target, held, came, went):
+        def arrival(n):
+            return pltpu.make_async_copy(
+                source.at[pl.ds(n * some, some)], held.at[pl.ds(n * some, some)], came.at[n]
+            )
+
+        def departure(n, p):
+            return pltpu.make_async_copy(
+                held.at[pl.ds(n * some, some), :, pl.ds(p * part, part)],
+                target.at[p, pl.ds(n * some, some)],
+                went.at[n, p],
+            )
+
+        for n in range(steps):
+            arrival(n).start()
+        for n in range(steps):
+            arrival(n).wait()
+            for p in range(pieces):
+                departure(n, p).start()
+        for n in range(steps):
+            for p in range(pieces):
+                departure(n, p).wait()
+
+    return pl.pallas_call(
+        kernel,
+        out_shape=jax.ShapeDtypeStruct((pieces, blocks, rows, part), array.dtype),
         in_specs=[pl.BlockSpec(memory_space=pltpu.HBM)],
-        out_specs=pl.BlockSpec(memory_space=pltpu.VMEM),
-        scratch_shapes=[pltpu.SemaphoreType.DMA((pieces,))],
+        out_specs=pl.BlockSpec(memory_space=pl.ANY),
+        scratch_shapes=[
+            pltpu.VMEM(array.shape, array.dtype),
+            pltpu.SemaphoreType.DMA((steps,)),
+            pltpu.SemaphoreType.DMA((steps, pieces)),
+        ],
         compiler_params=pltpu.CompilerParams(vmem_limit_bytes=8 * mib),
         cost_estimate=pl.CostEstimate(
             flops=0, bytes_accessed=2 * array.size * array.dtype.itemsize, transcendentals=0

time: 213 us -> 213 us (level)
  no operation moved by 1% of the time
where the time goes in v7:
time: 213 us
  blocking collectives  166 us (78%)
  starting transfers between devices  26.2 us (12%)
  waiting for transfers between devices  11.1 us (5%)
  Pallas kernels  7.03 us (3%)
    all_to_all x6, blocking collectives, exchange(): return lax.all_to_all(array, axes, split_axis=0, concat_axis=0, tiled=True)  166 us
    ppermute x1, starting transfers between devices, in_turn(): turn = lax.ppermute(array[0, 0], ('z', 'core'), pairs)  21.4 us
    all_to_all x1, waiting for transfers between devices, exchange(): return lax.all_to_all(array, axes, split_axis=0, concat_axis=0, tiled=True)  9.7 us
    all_to_all x1, starting transfers between devices, exchange(): return lax.all_to_all(array, axes, split_axis=0, concat_axis=0, tiled=True)  4.85 us
  transfers between devices with their start and end apart: 2, of which 2 were waited for; matrix products, arithmetic and copies ran while one was open for 0% of the time, Pallas kernels for 0%

profile of v7, /device:TPU:1, one launch (start us, length us, event | category | flops | bytes accessed | tf_op | source)
XLA Modules:
  0.0 213.0 jit_solution(14191534255044417848)
XLA Ops:
  0.0 2.1 shard_map.64
  2.1 4.9 %all-to-all-start = ((bf16[4,132,4,256]{3,2,1,0:T(4,128)(2,1)}), bf16[4,132,4,256]{3,2,1,0:T(4,128)(2,1)S(1)}, u32[]{:S(2)}, u32[]{:S(2)}) async-start(bf16[4,132,4,256]{3,2,1,0:T(4,128)(2,1)} %shard_map.64), calls=%async_computation | async-start | bytes 2162688 | tf_op jit(solution)/shard_map/all_to_all | solution.py:22
  7.0 0.2 convert_reduce_fusion
  7.2 9.7 %all-to-all-done = bf16[4,132,4,256]{3,2,1,0:T(4,128)(2,1)S(1)} async-done(((bf16[4,132,4,256]{3,2,1,0:T(4,128)(2,1)}), bf16[4,132,4,256]{3,2,1,0:T(4,128)(2,1)S(1)}, u32[]{:S(2)}, u32[]{:S(2)}) %all-to-all-start) | async-done | bytes 1081376 | tf_op jit(solution)/shard_map/all_to_all | solution.py:22
  16.9 0.7 reduce_sum.22
  17.6 0.1 pad
  17.8 0.3 convolution_convert_fusion
  18.1 0.4 reshape.74
  18.5 17.7 %all_to_all.35 = bf16[2,128,4,256]{3,2,1,0:T(4,128)(2,1)S(1)} all-to-all(bf16[2,128,4,256]{3,2,1,0:T(4,128)(2,1)S(1)} %reshape.74), channel_id=1, replica_groups=mesh['dp'=4,'half'=4,'z'=32,'core'=2] {'core'}, dimensions={0} | all-to-all | bytes 1048576 | tf_op jit(solution)/shard_map/all_to_all | solution.py:22
  36.2 0.2 copy.18
  36.4 21.4 %collective-permute-start = (bf16[4,256]{1,0:T(4,128)(2,1)S(1)}, bf16[4,256]{1,0:T(4,128)(2,1)S(1)}, u32[]{:S(2)}, u32[]{:S(2)}) collective-permute-start(bf16[4,256]{1,0:T(4,128)(2,1)S(1)} %slice_bitcast_fusion), channel_id=1, source_target_pairs={{1,33},{3,35},{5,37},{7,39},{9,41},{11,43},{13,45},{15,47},{17,49}... | collective-permute-start | bytes 6152 | tf_op jit(solution)/shard_map/ppermute | solution.py:36
  57.8 1.4 collective-permute-done.after
  59.2 69.4 %all_to_all.36 = bf16[128,2,4,256]{3,2,1,0:T(4,128)(2,1)S(1)} all-to-all(bf16[128,2,4,256]{3,2,1,0:T(4,128)(2,1)S(1)} %bitcast.26), channel_id=1, replica_groups=mesh['dp'=4,'half'=4,'z'=32,'core'=2] {'half','z'}, dimensions={0} | all-to-all | bytes 1048576 | tf_op jit(solution)/shard_map/all_to_all | solution.py:22
  128.6 0.1 reshape.75.block
  128.8 0.8 shard_map.65
  129.6 9.5 %all_to_all.37.projected = bf16[4,256,256]{2,1,0:T(8,128)(2,1)S(1)} all-to-all(bf16[4,256,256]{2,1,0:T(8,128)(2,1)S(1)} %shard_map.65), channel_id=1, replica_groups=mesh['dp'=4,'half'=4,'z'=32,'core'=2] {'dp'}, dimensions={0} | all-to-all | bytes 1048576 | tf_op jit(solution)/shard_map/all_to_all | solution.py:22
  139.0 2.0 shard_map.66
  141.0 9.6 %all_to_all.38 = bf16[4,256,256]{2,1,0:T(8,128)(2,1)S(1)} all-to-all(bf16[4,256,256]{2,1,0:T(8,128)(2,1)S(1)} %shard_map.66), channel_id=1, replica_groups=mesh['dp'=4,'half'=4,'z'=32,'core'=2] {'dp'}, dimensions={0} | all-to-all | bytes 1048576 | tf_op jit(solution)/shard_map/all_to_all | solution.py:22
  150.7 0.7 shard_map.67
  151.4 0.1 reshape.77
  151.5 56.0 %all_to_all.39 = bf16[128,2,4,256]{3,2,1,0:T(4,128)(2,1)S(1)} all-to-all(bf16[128,2,4,256]{3,2,1,0:T(4,128)(2,1)S(1)} %reshape.77), channel_id=1, replica_groups=mesh['dp'=4,'half'=4,'z'=32,'core'=2] {'half','z'}, dimensions={0} | all-to-all | bytes 1048576 | tf_op jit(solution)/shard_map/all_to_all | solution.py:22
  207.5 0.2 copy.15
  207.7 3.8 %all_to_all.40 = bf16[2,128,4,256]{3,2,1,0:T(4,128)(2,1)S(1)} all-to-all(bf16[2,128,4,256]{3,2,1,0:T(4,128)(2,1)S(1)} %copy.15), channel_id=1, replica_groups=mesh['dp'=4,'half'=4,'z'=32,'core'=2] {'core'}, dimensions={0} | all-to-all | bytes 1048576 | tf_op jit(solution)/shard_map/all_to_all | solution.py:22
  211.5 1.4 shard_map.68
  (13 shorter events, 0.1 us)
Async XLA Ops:
  2.1 4.9 %copy-start.4 = (s32[132,1]{0,1:T(1,128)S(1)}, s32[132,1]{0,1:T(1,128)}, u32[]{:S(2)}) copy-start(s32[132,1]{0,1:T(1,128)} %param.7) | copy-start | bytes 1588
  2.1 14.8 %all-to-all-start = ((bf16[4,132,4,256]{3,2,1,0:T(4,128)(2,1)}), bf16[4,132,4,256]{3,2,1,0:T(4,128)(2,1)S(1)}, u32[]{:S(2)}, u32[]{:S(2)}) async-start(bf16[4,132,4,256]{3,2,1,0:T(4,128)(2,1)} %shard_map.64), calls=%async_computation | async-start | bytes 2162688 | tf_op jit(solution)/shard_map/all_to_all | solution.py:22
  36.4 92.4 %copy-start = (bf16[1,1024,1024]{2,1,0:T(8,128)(2,1)S(1)}, bf16[1,1024,1024]{2,1,0:T(8,128)(2,1)}, u32[]{:S(2)}) copy-start(bf16[1,1024,1024]{2,1,0:T(8,128)(2,1)} %param.8) | copy-start | bytes 6291460
  36.4 22.8 %collective-permute-start = (bf16[4,256]{1,0:T(4,128)(2,1)S(1)}, bf16[4,256]{1,0:T(4,128)(2,1)S(1)}, u32[]{:S(2)}, u32[]{:S(2)}) collective-permute-start(bf16[4,256]{1,0:T(4,128)(2,1)S(1)} %slice_bitcast_fusion), channel_id=1, source_target_pairs={{1,33},{3,35},{5,37},{7,39},{9,41},{11,43},{13,45},{15,47},{17,49}... | collective-permute-start | bytes 6152 | tf_op jit(solution)/shard_map/ppermute | solution.py:36
  128.8 10.3 %copy-start.1 = (bf16[1,1024,1024]{2,1,0:T(8,128)(2,1)S(1)}, bf16[1,1024,1024]{2,1,0:T(8,128)(2,1)}, u32[]{:S(2)}) copy-start(bf16[1,1024,1024]{2,1,0:T(8,128)(2,1)} %param.9) | copy-start | bytes 6291460
  129.5 9.5 %copy-start.2 = (bf16[1,256,1024]{2,1,0:T(8,128)(2,1)S(1)}, bf16[1,256,1024]{2,1,0:T(8,128)(2,1)}, u32[]{:S(2)}) copy-start(bf16[1,256,1024]{2,1,0:T(8,128)(2,1)} %param.10) | copy-start | bytes 1572868
  129.5 9.5 %copy-start.3 = (bf16[1,256,1024]{2,1,0:T(8,128)(2,1)S(1)}, bf16[1,256,1024]{2,1,0:T(8,128)(2,1)}, u32[]{:S(2)}) copy-start(bf16[1,256,1024]{2,1,0:T(8,128)(2,1)} %param.11) | copy-start | bytes 1572868

commit v8 on v7

--- a/solution.py
+++ b/solution.py
@@ -30,10 +30,16 @@
     return ((owner_ids % cores) * ranks + ranking) * depth + owner_ids // cores
 
 
-def in_turn(array, depth):
-    away = depth // 2
-    pairs = [(z * cores + 1, (z + away) % depth * cores + 1) for z in range(depth)]
-    turn = lax.ppermute(array[0, 0], ("z", "core"), pairs)
+def in_turn(array, halves, depth):
+    def core_1(half, z):
+        return (half % halves * depth + z % depth) * cores + 1
+
+    pairs = [
+        (core_1(half, z), core_1(half + halves // 2, z + depth // 2))
+        for half in range(halves)
+        for z in range(depth)
+    ]
+    turn = lax.ppermute(array[0, 0], ("half", "z", "core"), pairs)
     return lax.optimization_barrier((array, turn))
 
 
@@ -226,7 +232,7 @@
         preferred_element_type=jnp.float32,
     ).astype(jnp.bfloat16)
     arrived = exchange(packed.reshape(cores, slots, piece_rows, quarter), "core")
-    arrived, turn = in_turn(jnp.moveaxis(arrived, 1, 0), depth)
+    arrived, turn = in_turn(jnp.moveaxis(arrived, 1, 0), halves, depth)
     block = exchange(arrived, ("half", "z"))
 
     projected = exchange(

time: 213 us -> 210 us (0.986)
  blocking collectives: 166 us -> 160 us
  starting transfers between devices: 26.2 us -> 28.8 us
    all_to_all x6, blocking collectives: 166 us -> 160 us  [exchange(): return lax.all_to_all(array, axes, split_axis=0, concat_axis=0, tiled=True)]
    ppermute x1, starting transfers between devices: 21.4 us -> 24 us  [in_turn(): turn = lax.ppermute(array[0, 0], ('half', 'z', 'core'), pairs)]
where the time goes in v8:
time: 210 us
  blocking collectives  160 us (76%)
  starting transfers between devices  28.8 us (14%)
  waiting for transfers between devices  10.9 us (5%)
  Pallas kernels  7.04 us (3%)
    all_to_all x6, blocking collectives, exchange(): return lax.all_to_all(array, axes, split_axis=0, concat_axis=0, tiled=True)  160 us
    ppermute x1, starting transfers between devices, in_turn(): turn = lax.ppermute(array[0, 0], ('half', 'z', 'core'), pairs)  24 us
    all_to_all x1, waiting for transfers between devices, exchange(): return lax.all_to_all(array, axes, split_axis=0, concat_axis=0, tiled=True)  9.7 us
    all_to_all x1, starting transfers between devices, exchange(): return lax.all_to_all(array, axes, split_axis=0, concat_axis=0, tiled=True)  4.85 us
  transfers between devices with their start and end apart: 2, of which 2 were waited for; matrix products, arithmetic and copies ran while one was open for 0% of the time, Pallas kernels for 0%

profile of v8, /device:TPU:1, one launch (start us, length us, event | category | flops | bytes accessed | tf_op | source)
XLA Modules:
  0.0 209.6 jit_solution(10841935001020999410)
XLA Ops:
  0.0 2.1 %shard_map.64 = bf16[4,132,4,256]{3,2,1,0:T(4,128)(2,1)} custom-call(bf16[132,4,1024]{2,1,0:T(4,128)(2,1)} %bitcast.30), custom_call_target="tpu_custom_call" | custom-call | bytes 2162688 | tf_op jit(solution)/shard_map/pallas_call | solution.py:76
  2.1 4.9 %all-to-all-start = ((bf16[4,132,4,256]{3,2,1,0:T(4,128)(2,1)}), bf16[4,132,4,256]{3,2,1,0:T(4,128)(2,1)S(1)}, u32[]{:S(2)}, u32[]{:S(2)}) async-start(bf16[4,132,4,256]{3,2,1,0:T(4,128)(2,1)} %shard_map.64), calls=%async_computation | async-start | bytes 2162688 | tf_op jit(solution)/shard_map/all_to_all | solution.py:22
  7.0 0.2 convert_reduce_fusion
  7.2 9.7 %all-to-all-done = bf16[4,132,4,256]{3,2,1,0:T(4,128)(2,1)S(1)} async-done(((bf16[4,132,4,256]{3,2,1,0:T(4,128)(2,1)}), bf16[4,132,4,256]{3,2,1,0:T(4,128)(2,1)S(1)}, u32[]{:S(2)}, u32[]{:S(2)}) %all-to-all-start) | async-done | bytes 1081376 | tf_op jit(solution)/shard_map/all_to_all | solution.py:22
  16.9 0.7 reduce_sum.22
  17.6 0.1 pad
  17.8 0.3 convolution_convert_fusion
  18.1 0.4 reshape.74
  18.5 17.7 %all_to_all.35 = bf16[2,128,4,256]{3,2,1,0:T(4,128)(2,1)S(1)} all-to-all(bf16[2,128,4,256]{3,2,1,0:T(4,128)(2,1)S(1)} %reshape.74), channel_id=1, replica_groups=mesh['dp'=4,'half'=4,'z'=32,'core'=2] {'core'}, dimensions={0} | all-to-all | bytes 1048576 | tf_op jit(solution)/shard_map/all_to_all | solution.py:22
  36.2 0.2 copy.18
  36.4 24.0 %collective-permute-start = (bf16[4,256]{1,0:T(4,128)(2,1)S(1)}, bf16[4,256]{1,0:T(4,128)(2,1)S(1)}, u32[]{:S(2)}, u32[]{:S(2)}) collective-permute-start(bf16[4,256]{1,0:T(4,128)(2,1)S(1)} %slice_bitcast_fusion), channel_id=1, source_target_pairs={{1,161},{3,163},{5,165},{7,167},{9,169},{11,171},{13,173},{15,175}... | collective-permute-start | bytes 6152 | tf_op jit(solution)/shard_map/ppermute | solution.py:42
  60.4 1.2 collective-permute-done.after
  61.6 68.2 %all_to_all.36 = bf16[128,2,4,256]{3,2,1,0:T(4,128)(2,1)S(1)} all-to-all(bf16[128,2,4,256]{3,2,1,0:T(4,128)(2,1)S(1)} %bitcast.26), channel_id=1, replica_groups=mesh['dp'=4,'half'=4,'z'=32,'core'=2] {'half','z'}, dimensions={0} | all-to-all | bytes 1048576 | tf_op jit(solution)/shard_map/all_to_all | solution.py:22
  129.8 0.1 reshape.75.block
  129.9 0.8 shard_map.65
  130.7 9.5 %all_to_all.37.projected = bf16[4,256,256]{2,1,0:T(8,128)(2,1)S(1)} all-to-all(bf16[4,256,256]{2,1,0:T(8,128)(2,1)S(1)} %shard_map.65), channel_id=1, replica_groups=mesh['dp'=4,'half'=4,'z'=32,'core'=2] {'dp'}, dimensions={0} | all-to-all | bytes 1048576 | tf_op jit(solution)/shard_map/all_to_all | solution.py:22
  140.2 2.0 shard_map.66
  142.2 9.6 %all_to_all.38 = bf16[4,256,256]{2,1,0:T(8,128)(2,1)S(1)} all-to-all(bf16[4,256,256]{2,1,0:T(8,128)(2,1)S(1)} %shard_map.66), channel_id=1, replica_groups=mesh['dp'=4,'half'=4,'z'=32,'core'=2] {'dp'}, dimensions={0} | all-to-all | bytes 1048576 | tf_op jit(solution)/shard_map/all_to_all | solution.py:22
  151.8 0.7 shard_map.67
  152.6 0.1 reshape.77
  152.7 51.5 %all_to_all.39 = bf16[128,2,4,256]{3,2,1,0:T(4,128)(2,1)S(1)} all-to-all(bf16[128,2,4,256]{3,2,1,0:T(4,128)(2,1)S(1)} %reshape.77), channel_id=1, replica_groups=mesh['dp'=4,'half'=4,'z'=32,'core'=2] {'half','z'}, dimensions={0} | all-to-all | bytes 1048576 | tf_op jit(solution)/shard_map/all_to_all | solution.py:22
  204.2 0.2 copy.15
  204.4 3.8 %all_to_all.40 = bf16[2,128,4,256]{3,2,1,0:T(4,128)(2,1)S(1)} all-to-all(bf16[2,128,4,256]{3,2,1,0:T(4,128)(2,1)S(1)} %copy.15), channel_id=1, replica_groups=mesh['dp'=4,'half'=4,'z'=32,'core'=2] {'core'}, dimensions={0} | all-to-all | bytes 1048576 | tf_op jit(solution)/shard_map/all_to_all | solution.py:22
  208.1 1.4 shard_map.68
  (13 shorter events, 0.1 us)
Async XLA Ops:
  2.1 4.9 %copy-start.4 = (s32[132,1]{0,1:T(1,128)S(1)}, s32[132,1]{0,1:T(1,128)}, u32[]{:S(2)}) copy-start(s32[132,1]{0,1:T(1,128)} %param.7) | copy-start | bytes 1588
  2.1 14.8 %all-to-all-start = ((bf16[4,132,4,256]{3,2,1,0:T(4,128)(2,1)}), bf16[4,132,4,256]{3,2,1,0:T(4,128)(2,1)S(1)}, u32[]{:S(2)}, u32[]{:S(2)}) async-start(bf16[4,132,4,256]{3,2,1,0:T(4,128)(2,1)} %shard_map.64), calls=%async_computation | async-start | bytes 2162688 | tf_op jit(solution)/shard_map/all_to_all | solution.py:22
  36.4 93.5 %copy-start = (bf16[1,1024,1024]{2,1,0:T(8,128)(2,1)S(1)}, bf16[1,1024,1024]{2,1,0:T(8,128)(2,1)}, u32[]{:S(2)}) copy-start(bf16[1,1024,1024]{2,1,0:T(8,128)(2,1)} %param.8) | copy-start | bytes 6291460
  36.4 25.2 %collective-permute-start = (bf16[4,256]{1,0:T(4,128)(2,1)S(1)}, bf16[4,256]{1,0:T(4,128)(2,1)S(1)}, u32[]{:S(2)}, u32[]{:S(2)}) collective-permute-start(bf16[4,256]{1,0:T(4,128)(2,1)S(1)} %slice_bitcast_fusion), channel_id=1, source_target_pairs={{1,161},{3,163},{5,165},{7,167},{9,169},{11,171},{13,173},{15,175}... | collective-permute-start | bytes 6152 | tf_op jit(solution)/shard_map/ppermute | solution.py:42
  129.9 10.3 %copy-start.1 = (bf16[1,1024,1024]{2,1,0:T(8,128)(2,1)S(1)}, bf16[1,1024,1024]{2,1,0:T(8,128)(2,1)}, u32[]{:S(2)}) copy-start(bf16[1,1024,1024]{2,1,0:T(8,128)(2,1)} %param.9) | copy-start | bytes 6291460
  130.7 9.5 %copy-start.2 = (bf16[1,256,1024]{2,1,0:T(8,128)(2,1)S(1)}, bf16[1,256,1024]{2,1,0:T(8,128)(2,1)}, u32[]{:S(2)}) copy-start(bf16[1,256,1024]{2,1,0:T(8,128)(2,1)} %param.10) | copy-start | bytes 1572868
  130.7 9.5 %copy-start.3 = (bf16[1,256,1024]{2,1,0:T(8,128)(2,1)S(1)}, bf16[1,256,1024]{2,1,0:T(8,128)(2,1)}, u32[]{:S(2)}) copy-start(bf16[1,256,1024]{2,1,0:T(8,128)(2,1)} %param.11) | copy-start | bytes 1572868
